TPU v7x, 256 devices: a whole 4x4x8 slice. The times are simulated.
256 devices in a mesh: space: 64 (over x, z_hi, y), batch: 4 (over z_lo, core).
Axes of the slice: x: 4, y: 4, z: 8 (z_hi: 4, z_lo: 2; z = z_hi * 2 + z_lo), core: 2. Of those that a mesh axis runs over, the one named last changes fastest.
Arguments:
- volumes: bfloat16 [8, 4, 256, 16, 256], P('batch', None, 'space'), may hold values from -6 to 6
- first_kernel: bfloat16 [16, 4, 3, 3, 3], replicated, may hold values from -0.625 to 0.625
- second_kernel: bfloat16 [32, 16, 3, 3, 3], replicated, may hold values from -0.875 to 0.875
- cotangent: bfloat16 [8, 32, 128, 8, 128], P('batch', None, 'space'), may hold values from -6 to 6
Outputs:
- activation: bfloat16 [8, 32, 128, 8, 128], P('batch', None, 'space')
- pooled_grad: bfloat16 [8, 16, 128, 8, 128], P('batch', None, 'space')
- first_grad: float32 [16, 4, 3, 3, 3], replicated
- second_grad: float32 [32, 16, 3, 3, 3], replicated
All inputs are finite; a program needn't handle non-finite values.
Results may differ from a plain program's by a relative error of at most 0.0057.
Values may be sent and summed in bfloat16 or wider, within the bound.
A program may use at most 192 MiB of HBM per device.

v0:
```python
import functools
import math

import jax
import jax.numpy as jnp
from jax import lax
from jax.experimental import pallas as pl
from jax.experimental.pallas import tpu as pltpu
from jax.sharding import PartitionSpec as P

F32 = jnp.float32
BF16 = jnp.bfloat16
MESH = pl.DeviceIdType.MESH


def space_grid(count):
    side = round(count ** (1 / 3))
    if side**3 == count:
        return side, side, side
    return 2, 1, count // 2


def dot(a, b):
    return jnp.dot(a, b, preferred_element_type=F32)


def dot_nt(a, b):
    return lax.dot_general(a, b, (((1,), (1,)), ((), ())), preferred_element_type=F32)


def shifts(v):
    lanes = lax.broadcasted_iota(jnp.int32, v.shape, 1)
    width = v.shape[1]
    before = jnp.where(lanes == 0, 0.0, pltpu.roll(v, 1, 1))
    after = jnp.where(lanes == width - 1, 0.0, pltpu.roll(v, width - 1, 1))
    return before, after


def split(v):
    high = v.astype(BF16)
    return high, (v - high.astype(F32)).astype(BF16)


def act_and_slope(z):
    t = jnp.tanh(0.5 * z)
    a = 0.65 + 0.35 * t
    return z * a, a + (0.175 * z) * (1.0 - t * t)


def kernel(
    sizes, scales, vol, w1, w2, cot, out_act, out_pg, out_g1, out_g2,
    vbuf, vf, u1, slope, pb, ph, u2, cotb, cotf, actf, actb, db, dh, u3, bkf, bkb,
    a1s, a2s, w2f, a1, a2, a3, acc1, acc2, pack, r1, r2, res, flat,
    local_sem, halo_send, halo_recv, sum_send, sum_recv,
):
    (nx, nzh, ny), nb = sizes
    n_space = nx * nzh * ny
    g1, g2 = nx * ny, nzh * nb
    tp = 16 // g1
    sp, bt = lax.axis_index("space"), lax.axis_index("batch")
    xi = lax.div(sp, nzh * ny)
    zi = lax.rem(lax.div(sp, ny), nzh)
    yi = lax.rem(sp, ny)
    i1 = xi * ny + yi
    i2 = zi * nb + bt
    right = lax.rem(sp + 1, n_space)
    left = lax.rem(sp + n_space - 1, n_space)

    def peer1(p):
        return (lax.div(p, ny) * (nzh * ny) + zi * ny + lax.rem(p, ny), bt)

    def peer2(p):
        return (xi * (nzh * ny) + lax.div(p, nb) * ny + yi, lax.rem(p, nb))

    barrier = pltpu.get_barrier_semaphore()
    for side in (left, right):
        pl.semaphore_signal(barrier, inc=1, device_id=(side, bt), device_id_type=MESH)

    def greet1(d, c):
        pl.semaphore_signal(barrier, inc=1, device_id=peer1(lax.rem(i1 + d, g1)), device_id_type=MESH)
        return c

    def greet2(d, c):
        pl.semaphore_signal(barrier, inc=1, device_id=peer2(lax.rem(i2 + d, g2)), device_id_type=MESH)
        return c

    lax.fori_loop(1, g1, greet1, 0)
    lax.fori_loop(1, g2, greet2, 0)

    own = []
    for s in range(2):
        for x in range(4):
            own.append(pltpu.make_async_copy(vol.at[s, :, x], vbuf.at[s, x + 1], local_sem.at[s * 4 + x]))
    own.append(pltpu.make_async_copy(cot, cotb, local_sem.at[8]))
    for c in own:
        c.start()

    pl.semaphore_wait(barrier, 2 + g1 - 1 + g2 - 1)

    def both_ways(k, to_right, land_right, to_left, land_left):
        one = pltpu.make_async_remote_copy(
            src_ref=to_right, dst_ref=land_right, send_sem=halo_send.at[k, 0], recv_sem=halo_recv.at[k, 0],
            device_id=(right, bt), device_id_type=MESH,
        )
        two = pltpu.make_async_remote_copy(
            src_ref=to_left, dst_ref=land_left, send_sem=halo_send.at[k, 1], recv_sem=halo_recv.at[k, 1],
            device_id=(left, bt), device_id_type=MESH,
        )
        return one, two

    halos = [both_ways(s, vol.at[s, :, 3], vbuf.at[s, 0], vol.at[s, :, 0], vbuf.at[s, 5]) for s in range(2)]
    for pair in halos:
        for c in pair:
            c.start()

    def arrive(pair, low, high):
        for c in pair:
            c.wait()

        @pl.when(sp == 0)
        def _():
            low[...] = jnp.zeros_like(low)

        @pl.when(sp == n_space - 1)
        def _():
            high[...] = jnp.zeros_like(high)

    a1s[...] = jnp.zeros_like(a1s)
    for kx in range(3):
        for ky in range(3):
            for kz in range(3):
                row = ky * 80 + kz * 24 + kx * 4
                a1s[row : row + 4, 0:16] = w1[kx, ky, kz].astype(F32)
    base = a1s[...]
    t1 = base
    for x in range(1, 4):
        t1 = t1 + pltpu.roll(pltpu.roll(base, 4 * x, 0), 16 * x, 1)
    a1[...] = t1.T[0:64].astype(BF16)

    w2f[...] = jnp.zeros_like(w2f)
    w2f[:, 0:32] = w2[...].reshape(432, 32).astype(F32)
    a2s[...] = jnp.zeros_like(a2s)
    for ky in range(3):
        for kx in range(3):
            a2s[ky * 192 + kx * 48 : ky * 192 + kx * 48 + 48, :] = w2f[(kx * 3 + ky) * 48 : (kx * 3 + ky) * 48 + 48, :]
    base = a2s[...]
    t2 = base + pltpu.roll(pltpu.roll(base, 48, 0), 32, 1)
    a2[...] = t2.T[0:64].astype(BF16)
    for ky in range(3):
        for kz in range(3):
            rows = [((kx * 3 + 2 - ky) * 3 + 2 - kz) * 16 for kx in range(3)]
            blocks = [w2f[r : r + 16, :] for r in rows]
            first = blocks[2] + pltpu.roll(blocks[1], 32, 1) + pltpu.roll(blocks[0], 64, 1)
            both = jnp.concatenate([first, pltpu.roll(first, 32, 1)], axis=0)
            a3[:, (ky * 3 + kz) * 128 : (ky * 3 + kz) * 128 + 128] = both.astype(BF16)

    zrow = lax.broadcasted_iota(jnp.int32, (256, 128), 0)
    zcol = lax.broadcasted_iota(jnp.int32, (256, 128), 1)
    halve = jnp.where(lax.div(zrow, 2) == zcol, 0.125, 0.0).astype(BF16)
    zrow = lax.broadcasted_iota(jnp.int32, (128, 256), 0)
    zcol = lax.broadcasted_iota(jnp.int32, (128, 256), 1)
    double = jnp.where(zrow == lax.div(zcol, 2), 1.0, 0.0).astype(BF16)

    acc1[...] = jnp.zeros_like(acc1)
    acc2[...] = jnp.zeros_like(acc2)
    for s in range(2):
        u1[s, 0:80, :] = jnp.zeros((80, 256), BF16)
        u1[s, 1360:1456, :] = jnp.zeros((96, 256), BF16)
        u2[s, 0:192, :] = jnp.zeros((192, 128), BF16)
        u2[s, 1728:1984, :] = jnp.zeros((256, 128), BF16)
        u3[s, 0:384, :] = jnp.zeros((384, 128), BF16)
        u3[s, 3456:3840, :] = jnp.zeros((384, 128), BF16)

    def stage1(s):
        for c in own[s * 4 : s * 4 + 4]:
            c.wait()
        arrive(halos[s], vbuf.at[s, 0], vbuf.at[s, 5])
        planes = vbuf[s].reshape(384, 256).astype(F32)
        for half in range(2):
            vf[half] = planes[:, 128 * half : 128 * half + 128]

        def fill(y, c):
            v = jnp.concatenate([vf[half, pl.ds(y, 24, stride=16), :] for half in range(2)], axis=1)
            before, after = shifts(v)
            rows = jnp.concatenate([before, v, after, jnp.zeros((8, 256), F32)], axis=0)
            u1[s, pl.ds(pl.multiple_of((y + 1) * 80, 16), 80), :] = rows.astype(BF16)
            return c

        lax.fori_loop(0, 16, fill, 0, unroll=4)

        def forward(j, c):
            total = None
            for i in range(2):
                y = 2 * j + i
                pre = dot(a1[...], u1[s, pl.ds(pl.multiple_of(y * 80, 16), 256), :])
                act, sl = act_and_slope(pre)
                slope[s, pl.ds(pl.multiple_of(y * 64, 64), 64), :] = 0.125 * sl
                total = act if total is None else total + act
            pairs = jnp.concatenate([total[0:16] + total[16:32], total[32:48] + total[48:64]], axis=0)
            high, low = split(pairs)
            pooled = (dot(high, halve) + dot(low, halve)).astype(BF16)
            pb[s, j] = pooled.reshape(2, 16, 128)
            mid = pooled.astype(F32)
            before, after = shifts(mid)
            for x in range(2):
                part = slice(16 * x, 16 * x + 16)
                rows = jnp.concatenate([before[part], mid[part], after[part]], axis=0)
                u2[s, pl.ds(pl.multiple_of((j + 1) * 192 + (x + 1) * 48, 16), 48), :] = rows.astype(BF16)
            return c

        lax.fori_loop(0, 8, forward, 0, unroll=4)
        pair = both_ways(2 + s, pb.at[s, :, 1], ph.at[s, 0], pb.at[s, :, 0], ph.at[s, 1])
        for c in pair:
            c.start()
        return pair

    def stage2(s, pair):
        if s == 0:
            own[8].wait()
        cotf[...] = cotb[s].reshape(512, 128).astype(F32)
        arrive(pair, ph.at[s, 0], ph.at[s, 1])

        def fill(j, c):
            for side in range(2):
                mid = ph[s, side, j].astype(F32)
                before, after = shifts(mid)
                rows = jnp.concatenate([before, mid, after], axis=0)
                u2[s, pl.ds(pl.multiple_of((j + 1) * 192 + side * 144, 16), 48), :] = rows.astype(BF16)
            return c

        lax.fori_loop(0, 8, fill, 0, unroll=4)

        def forward(j, c):
            pre = dot(a2[...], u2[s, pl.ds(pl.multiple_of(j * 192, 64), 640), :])
            act, sl = act_and_slope(pre)
            got = []
            for x in range(2):
                actf[pl.ds(x * 8 + j, 32, stride=16), :] = act[32 * x : 32 * x + 32]
                got.append(cotf[pl.ds(x * 8 + j, 32, stride=16), :])
            delta = (jnp.concatenate(got, axis=0) * sl).astype(BF16)
            db[s, j] = delta.reshape(2, 32, 128)
            mid = delta.astype(F32)
            before, after = shifts(mid)
            for kz, rows in enumerate((before, mid, after)):
                u3[s, pl.ds(pl.multiple_of((j + 1) * 384 + kz * 128 + 32, 32), 64), :] = rows.astype(BF16)
            return c

        lax.fori_loop(0, 8, forward, 0, unroll=4)
        out = both_ways(4 + s, db.at[s, :, 1], dh.at[s, 0], db.at[s, :, 0], dh.at[s, 1])
        for c in out:
            c.start()
        actb[s] = actf[...].reshape(32, 2, 8, 128).astype(BF16)
        act_copy = pltpu.make_async_copy(actb.at[s], out_act.at[s], local_sem.at[9 + s])
        act_copy.start()

        def grad(j, c):
            field = jnp.concatenate(
                [u2[s, pl.ds(pl.multiple_of((2 * j + i) * 192, 64), 576), :] for i in range(2)], axis=1
            )
            delta = jnp.concatenate([db[s, 2 * j + i].reshape(64, 128) for i in range(2)], axis=1)
            acc2[:, 0:64] += dot_nt(field, delta)
            return c

        lax.fori_loop(0, 4, grad, 0, unroll=2)
        return out, act_copy

    def stage3(s, pair):
        arrive(pair, dh.at[s, 0], dh.at[s, 1])

        def fill(j, c):
            for side in range(2):
                mid = dh[s, side, j].astype(F32)
                before, after = shifts(mid)
                for kz, rows in enumerate((before, mid, after)):
                    at = pl.multiple_of((j + 1) * 384 + kz * 128 + side * 96, 32)
                    u3[s, pl.ds(at, 32), :] = rows.astype(BF16)
            return c

        lax.fori_loop(0, 8, fill, 0, unroll=4)

        def backward(j, c):
            back = dot(a3[...], u3[s, pl.ds(pl.multiple_of(j * 384, 128), 1152), :])
            for x in range(2):
                bkf[pl.ds(x * 8 + j, 16, stride=16), :] = back[16 * x : 16 * x + 16]
            high, low = split(back)
            up = dot(high, double) + dot(low, double)
            up = jnp.concatenate([up[0:16], up[0:16], up[16:32], up[16:32]], axis=0)
            fields, deltas = [], []
            for i in range(2):
                y = 2 * j + i
                deltas.append((up * slope[s, pl.ds(pl.multiple_of(y * 64, 64), 64), :]).astype(BF16))
                fields.append(u1[s, pl.ds(pl.multiple_of(y * 80, 16), 256), :])
            acc1[:, 0:64] += dot_nt(jnp.concatenate(fields, axis=1), jnp.concatenate(deltas, axis=1))
            return c

        lax.fori_loop(0, 8, backward, 0, unroll=4)
        bkb[s] = bkf[...].reshape(16, 2, 8, 128).astype(BF16)
        copy = pltpu.make_async_copy(bkb.at[s], out_pg.at[s], local_sem.at[11 + s])
        copy.start()
        return copy

    pooled_pairs = [stage1(0), stage1(1)]
    second = [stage2(s, pooled_pairs[s]) for s in range(2)]
    third = [stage3(s, second[s][0]) for s in range(2)]

    lanes = lax.broadcasted_iota(jnp.int32, (432, 128), 1)
    g = acc2[...].reshape(3, 192, 128)
    upper = g[:, 48:192].reshape(432, 128)
    f2 = jnp.where(lanes < 32, g[:, 0:144].reshape(432, 128) + pltpu.roll(upper, 96, 1), 0.0)
    g = acc1[0:240, :]
    f1 = g
    for x in range(1, 4):
        f1 = f1 + pltpu.roll(pltpu.roll(g, 240 - 4 * x, 0), 128 - 16 * x, 1)
    rows = lax.rem(lax.broadcasted_iota(jnp.int32, (240, 128), 0), 80)
    f1 = jnp.where(lax.broadcasted_iota(jnp.int32, (240, 128), 1) < 16, f1, 0.0)
    f1c = None
    for kz in range(3):
        part = jnp.where((rows >= 24 * kz) & (rows < 24 * kz + 12), f1, 0.0)
        part = pltpu.roll(part, 240 - 12 * kz, 0) if kz else part
        f1c = part if f1c is None else f1c + part
    f1c = f1c.reshape(3, 80, 128)[:, 0:40].reshape(120, 128)
    f1c = jnp.concatenate([f1c, jnp.zeros((8, 128), F32)], axis=0)
    body = pltpu.roll(f1c, 96, 1)
    rest = []
    for ky in range(3):
        part = f2[ky * 144 : ky * 144 + 128]
        body = body + (pltpu.roll(part, 32 * ky, 1) if ky else part)
        rest.append(f2[ky * 144 + 128 : ky * 144 + 144])
    rest = jnp.concatenate(rest, axis=0)
    lanes = lanes[0:48]
    first = jnp.where(lanes < 16, rest, 0.0)
    last = jnp.where(lanes >= 16, rest, 0.0)
    extra = jnp.concatenate([pltpu.roll(first, 112, 1), pltpu.roll(last, 96, 1), jnp.zeros((32, 128), F32)], axis=0)
    pack[...] = (body + extra).reshape(16, 8, 128)

    def spread_out(phase, group, index, peer, src, dst):
        def make(d):
            other = lax.rem(index + d, group)
            return pltpu.make_async_remote_copy(
                src_ref=src(other), dst_ref=dst, send_sem=sum_send.at[phase, d], recv_sem=sum_recv.at[phase, d],
                device_id=peer(other), device_id_type=MESH,
            )

        def go(d, c):
            make(d).start()
            return c

        def end(d, c):
            make(d).wait()
            return c

        lax.fori_loop(1, group, go, 0)
        lax.fori_loop(1, group, end, 0)

    mine = pl.ds(i1 * tp, tp)
    r1[i1] = pack[mine]
    spread_out(0, g1, i1, peer1, lambda p: pack.at[pl.ds(p * tp, tp)], r1.at[i1])
    r2[i2] = jnp.sum(r1[...], axis=0)
    spread_out(1, g2, i2, peer2, lambda p: r2.at[i2], r2.at[i2])
    res[i1] = jnp.sum(r2[...], axis=0)
    spread_out(2, g1, i1, peer1, lambda p: res.at[i1], res.at[i1])

    total = res[...].reshape(128, 128)
    lanes = lax.broadcasted_iota(jnp.int32, (48, 128), 1)
    first = pltpu.roll(total[0:48], 16, 1)
    last = pltpu.roll(total[48:96], 32, 1)
    rest = jnp.where(lanes < 16, first, last) * scales[1]
    for ky in range(3):
        part = total * scales[1]
        part = pltpu.roll(part, 128 - 32 * ky, 1) if ky else part
        whole = jnp.concatenate([part, rest[ky * 16 : ky * 16 + 16]], axis=0)[:, 0:32]
        for kx in range(3):
            out_g2[kx, ky] = whole[kx * 48 : kx * 48 + 48].reshape(3, 16, 32)
    flat[...] = pltpu.roll(total, 32, 1) * scales[0]
    for kx in range(3):
        for ky in range(3):
            for kz in range(3):
                row = ky * 40 + kz * 12 + kx * 4
                out_g1[kx, ky, kz] = flat[row : row + 4, 0:16]

    for s in range(2):
        second[s][1].wait()
        third[s].wait()


def solution(mesh):
    sizes = (space_grid(mesh.shape["space"]), mesh.shape["batch"])

    def body(volumes, first_kernel, second_kernel, cotangent):
        cells = math.prod(volumes.shape) // volumes.shape[1] * mesh.size
        scales = (1.0 / math.sqrt(cells), 1.0 / math.sqrt(cells / 8))
        w1 = jnp.transpose(first_kernel, (2, 3, 4, 1, 0))
        w2 = jnp.transpose(second_kernel, (2, 3, 4, 1, 0))
        anywhere = pl.BlockSpec(memory_space=pl.ANY)
        vmem = pl.BlockSpec(memory_space=pltpu.VMEM)
        g1 = sizes[0][0] * sizes[0][2]
        g2 = sizes[0][1] * sizes[1]
        act, pooled_grad, grad1, grad2 = pl.pallas_call(
            functools.partial(kernel, sizes, scales),
            out_shape=(
                jax.ShapeDtypeStruct((2, 32, 2, 8, 128), BF16),
                jax.ShapeDtypeStruct((2, 16, 2, 8, 128), BF16),
                jax.ShapeDtypeStruct((3, 3, 3, 4, 16), F32),
                jax.ShapeDtypeStruct((3, 3, 3, 16, 32), F32),
            ),
            in_specs=[anywhere, vmem, vmem, anywhere],
            out_specs=(anywhere, anywhere, vmem, vmem),
            scratch_shapes=[
                pltpu.VMEM((2, 6, 4, 16, 256), BF16),
                pltpu.VMEM((2, 384, 128), F32),
                pltpu.VMEM((2, 1456, 256), BF16),
                pltpu.VMEM((2, 1024, 256), F32),
                pltpu.VMEM((2, 8, 2, 16, 128), BF16),
                pltpu.VMEM((2, 2, 8, 16, 128), BF16),
                pltpu.VMEM((2, 1984, 128), BF16),
                pltpu.VMEM((2, 32, 2, 8, 128), BF16),
                pltpu.VMEM((512, 128), F32),
                pltpu.VMEM((512, 128), F32),
                pltpu.VMEM((2, 32, 2, 8, 128), BF16),
                pltpu.VMEM((2, 8, 2, 32, 128), BF16),
                pltpu.VMEM((2, 2, 8, 32, 128), BF16),
                pltpu.VMEM((2, 3840, 128), BF16),
                pltpu.VMEM((256, 128), F32),
                pltpu.VMEM((2, 16, 2, 8, 128), BF16),
                pltpu.VMEM((256, 128), F32),
                pltpu.VMEM((640, 128), F32),
                pltpu.VMEM((432, 128), F32),
                pltpu.VMEM((64, 256), BF16),
                pltpu.VMEM((64, 640), BF16),
                pltpu.VMEM((32, 1152), BF16),
                pltpu.VMEM((256, 128), F32),
                pltpu.VMEM((576, 128), F32),
                pltpu.VMEM((16, 8, 128), F32),
                pltpu.VMEM((g1, 16 // g1, 8, 128), F32),
                pltpu.VMEM((g2, 16 // g1, 8, 128), F32),
                pltpu.VMEM((g1, 16 // g1, 8, 128), F32),
                pltpu.VMEM((128, 128), F32),
                pltpu.SemaphoreType.DMA((13,)),
                pltpu.SemaphoreType.DMA((6, 2)),
                pltpu.SemaphoreType.DMA((6, 2)),
                pltpu.SemaphoreType.DMA((3, max(g1, g2))),
                pltpu.SemaphoreType.DMA((3, max(g1, g2))),
            ],
            compiler_params=pltpu.CompilerParams(
                collective_id=0, has_side_effects=True, vmem_limit_bytes=40 * 1024 * 1024
            ),
        )(volumes, w1, w2, cotangent)
        return (
            act,
            pooled_grad,
            jnp.transpose(grad1, (4, 3, 0, 1, 2)),
            jnp.transpose(grad2, (4, 3, 0, 1, 2)),
        )

    return jax.shard_map(
        body,
        mesh=mesh,
        in_specs=(
            P("batch", None, "space", None, None),
            P(),
            P(),
            P("batch", None, "space", None, None),
        ),
        out_specs=(
            P("batch", None, "space", None, None),
            P("batch", None, "space", None, None),
            P(),
            P(),
        ),
        check_vma=False,
    )
```

profile of v0, /device:TPU:1, one launch (start us, length us, event | category | flops | bytes accessed | tf_op | source)
XLA Modules:
  0.0 64.2 jit_solution(788501138390602499)
XLA Ops:
  0.6 0.0 copy-start
  0.6 0.9 %copy-done = bf16[2,4,4,16,256]{4,3,2,1,0:T(8,128)(2,1)S(1)} copy-done((bf16[2,4,4,16,256]{4,3,2,1,0:T(8,128)(2,1)S(1)}, bf16[2,4,4,16,256]{4,3,2,1,0:T(8,128)(2,1)}, u32[]{:S(2)}) %copy-start) | copy-done | bytes 262168
  1.6 0.0 copy-start.1
  1.6 0.9 %copy-done.1 = bf16[2,32,2,8,128]{4,3,2,1,0:T(8,128)(2,1)S(1)} copy-done((bf16[2,32,2,8,128]{4,3,2,1,0:T(8,128)(2,1)S(1)}, bf16[2,32,2,8,128]{4,3,2,1,0:T(8,128)(2,1)}, u32[]{:S(2)}) %copy-start.1) | copy-done | bytes 262168
  2.5 0.0 copy-start.2
  2.5 0.9 %copy-done.2 = bf16[32,16,3,3,3]{0,1,4,3,2:T(8,128)(2,1)S(1)} copy-done((bf16[32,16,3,3,3]{0,1,4,3,2:T(8,128)(2,1)S(1)}, bf16[32,16,3,3,3]{0,1,4,3,2:T(8,128)(2,1)}, u32[]{:S(2)}) %copy-start.2) | copy-done | bytes 27672
  3.4 0.0 copy-start.3
  3.4 0.7 %copy-done.3 = bf16[16,4,3,3,3]{0,1,4,3,2:T(4,128)(2,1)S(1)} copy-done((bf16[16,4,3,3,3]{0,1,4,3,2:T(4,128)(2,1)S(1)}, bf16[16,4,3,3,3]{0,1,4,3,2:T(4,128)(2,1)}, u32[]{:S(2)}) %copy-start.3) | copy-done | bytes 3480
  4.2 57.4 %shard_map.75 = (bf16[2,32,2,8,128]{4,3,2,1,0:T(8,128)(2,1)S(1)}, bf16[2,16,2,8,128]{4,3,2,1,0:T(8,128)(2,1)S(1)}, f32[3,3,3,4,16]{4,3,2,1,0:T(4,128)S(1)}, f32[3,3,3,16,32]{4,3,2,1,0:T(8,128)S(1)}) custom-call(bf16[2,4,4,16,256]{4,3,2,1,0:T(8,128)(2,1)S(1)} %copy-done, bf16[3,3,3,4,16]{4,3,2,1,0:T(4,128)(2,1)S(1)} %bitcast.7, ...), custom_call_target="tpu_custom_call" | custom-call | tf_op jit(solution)/shard_map/pallas_call | solution.py:398
  61.6 0.7 %copy.12 = bf16[2,32,2,8,128]{4,3,2,1,0:T(8,128)(2,1)} copy(bf16[2,32,2,8,128]{4,3,2,1,0:T(8,128)(2,1)S(1)} %get-tuple-element.16) | data formatting | bytes 524288
  62.3 0.7 %copy.13 = bf16[2,16,2,8,128]{4,3,2,1,0:T(8,128)(2,1)} copy(bf16[2,16,2,8,128]{4,3,2,1,0:T(8,128)(2,1)S(1)} %get-tuple-element.17) | data formatting | bytes 262144
  62.9 0.6 copy.14
  63.6 0.7 %copy.15 = f32[32,16,3,3,3]{0,1,4,3,2:T(8,128)} copy(f32[32,16,3,3,3]{0,1,4,3,2:T(8,128)S(1)} %bitcast.4) | data formatting | bytes 110592
Async XLA Ops:
  0.6 1.0 %copy-start = (bf16[2,4,4,16,256]{4,3,2,1,0:T(8,128)(2,1)S(1)}, bf16[2,4,4,16,256]{4,3,2,1,0:T(8,128)(2,1)}, u32[]{:S(2)}) copy-start(bf16[2,4,4,16,256]{4,3,2,1,0:T(8,128)(2,1)} %vol.1) | copy-start | bytes 786436
  1.6 0.9 %copy-start.1 = (bf16[2,32,2,8,128]{4,3,2,1,0:T(8,128)(2,1)S(1)}, bf16[2,32,2,8,128]{4,3,2,1,0:T(8,128)(2,1)}, u32[]{:S(2)}) copy-start(bf16[2,32,2,8,128]{4,3,2,1,0:T(8,128)(2,1)} %cot.1) | copy-start | bytes 786436
  2.5 0.9 %copy-start.2 = (bf16[32,16,3,3,3]{0,1,4,3,2:T(8,128)(2,1)S(1)}, bf16[32,16,3,3,3]{0,1,4,3,2:T(8,128)(2,1)}, u32[]{:S(2)}) copy-start(bf16[32,16,3,3,3]{0,1,4,3,2:T(8,128)(2,1)} %param.6) | copy-start | bytes 82948
  3.4 0.7 %copy-start.3 = (bf16[16,4,3,3,3]{0,1,4,3,2:T(4,128)(2,1)S(1)}, bf16[16,4,3,3,3]{0,1,4,3,2:T(4,128)(2,1)}, u32[]{:S(2)}) copy-start(bf16[16,4,3,3,3]{0,1,4,3,2:T(4,128)(2,1)} %param.5) | copy-start | bytes 10372
where the time goes:
time: 64.5 us; the launch traced here: 64.2 us
  Pallas kernels  57.4 us (89%)
  local copies, waits for them, and re-layouts  6.2 us (10%)
  between operations  0.65 us (1%)
    pallas_call x1, Pallas kernels, body(): pl.pallas_call(functools.partial(kernel, sizes, scales), out_shape=(jax.S...  57.4 us
    unnamed x12, local copies, waits for them, and re-layouts  6.2 us

commit v1 on v0

v1 whole, which is shorter than its diff:
```python
import functools
import math

import jax
import jax.numpy as jnp
from jax import lax
from jax.experimental import pallas as pl
from jax.experimental.pallas import tpu as pltpu
from jax.sharding import PartitionSpec as P

F32 = jnp.float32
BF16 = jnp.bfloat16
MESH = pl.DeviceIdType.MESH


def space_grid(count):
    side = round(count ** (1 / 3))
    if side**3 == count:
        return side, side, side
    return 2, 1, count // 2


def dot(a, b):
    return jnp.dot(a, b, preferred_element_type=F32)


def dot_nt(a, b):
    return lax.dot_general(a, b, (((1,), (1,)), ((), ())), preferred_element_type=F32)


def shifts(v):
    lanes = lax.broadcasted_iota(jnp.int32, v.shape, 1)
    width = v.shape[1]
    before = jnp.where(lanes == 0, 0.0, pltpu.roll(v, 1, 1))
    after = jnp.where(lanes == width - 1, 0.0, pltpu.roll(v, width - 1, 1))
    return before, after


def split(v):
    high = v.astype(BF16)
    return high, (v - high.astype(F32)).astype(BF16)


def act_and_slope(z):
    t = jnp.tanh(0.5 * z)
    a = 0.65 + 0.35 * t
    return z * a, a + (0.175 * z) * (1.0 - t * t)


def kernel(
    sizes, vol, w1_hbm, w2_hbm, cot, out_act, out_pg, out_s1, out_s2,
    vbuf, vf, u1, slope, pb, ph, u2, cotb, ch, cotf, actf, actb, db, u3, bkf, bkb,
    w1, w2, a1s, a2s, w2f, a1, a2, a3, acc1, acc2, pack2, p1, q1, r1, r2, res,
    local_sem, halo_send, halo_recv, sum_send, sum_recv,
):
    (nx, nzh, ny), nb = sizes
    n_space = nx * nzh * ny
    g1, g2 = nx * ny, nzh * nb
    tp = 16 // g1
    sp, bt = lax.axis_index("space"), lax.axis_index("batch")
    xi = lax.div(sp, nzh * ny)
    zi = lax.rem(lax.div(sp, ny), nzh)
    yi = lax.rem(sp, ny)
    i1 = xi * ny + yi
    i2 = zi * nb + bt
    right = lax.rem(sp + 1, n_space)
    left = lax.rem(sp + n_space - 1, n_space)

    def peer1(p):
        return (lax.div(p, ny) * (nzh * ny) + zi * ny + lax.rem(p, ny), bt)

    def peer2(p):
        return (xi * (nzh * ny) + lax.div(p, nb) * ny + yi, lax.rem(p, nb))

    barrier = pltpu.get_barrier_semaphore()
    for side in (left, right):
        pl.semaphore_signal(barrier, inc=1, device_id=(side, bt), device_id_type=MESH)

    def greet1(d, c):
        pl.semaphore_signal(barrier, inc=1, device_id=peer1(lax.rem(i1 + d, g1)), device_id_type=MESH)
        return c

    def greet2(d, c):
        pl.semaphore_signal(barrier, inc=1, device_id=peer2(lax.rem(i2 + d, g2)), device_id_type=MESH)
        return c

    lax.fori_loop(1, g1, greet1, 0)
    lax.fori_loop(1, g2, greet2, 0)

    own = []
    for s in range(2):
        for x in range(4):
            own.append(pltpu.make_async_copy(vol.at[s, :, x], vbuf.at[s, x + 1], local_sem.at[s * 4 + x]))
    own.append(pltpu.make_async_copy(cot, cotb, local_sem.at[8]))
    own.append(pltpu.make_async_copy(w1_hbm, w1, local_sem.at[13]))
    own.append(pltpu.make_async_copy(w2_hbm, w2, local_sem.at[14]))
    for c in own:
        c.start()
    for c in own[0:8]:
        c.wait()

    pl.semaphore_wait(barrier, 2 + g1 - 1 + g2 - 1)

    def both_ways(k, to_right, land_right, to_left, land_left):
        one = pltpu.make_async_remote_copy(
            src_ref=to_right, dst_ref=land_right, send_sem=halo_send.at[k, 0], recv_sem=halo_recv.at[k, 0],
            device_id=(right, bt), device_id_type=MESH,
        )
        two = pltpu.make_async_remote_copy(
            src_ref=to_left, dst_ref=land_left, send_sem=halo_send.at[k, 1], recv_sem=halo_recv.at[k, 1],
            device_id=(left, bt), device_id_type=MESH,
        )
        return one, two

    halos = [both_ways(s, vbuf.at[s, 4], vbuf.at[s, 0], vbuf.at[s, 1], vbuf.at[s, 5]) for s in range(2)]
    for pair in halos:
        for c in pair:
            c.start()
    for c in own[8:]:
        c.wait()
    cot_pairs = [both_ways(4 + s, cotb.at[s, :, 1], ch.at[s, 0], cotb.at[s, :, 0], ch.at[s, 1]) for s in range(2)]
    for pair in cot_pairs:
        for c in pair:
            c.start()

    def arrive(pair, low, high):
        for c in pair:
            c.wait()

        @pl.when(sp == 0)
        def _():
            low[...] = jnp.zeros_like(low)

        @pl.when(sp == n_space - 1)
        def _():
            high[...] = jnp.zeros_like(high)

    a1s[...] = jnp.zeros_like(a1s)
    for kx in range(3):
        for ky in range(3):
            for kz in range(3):
                row = ky * 80 + kz * 24 + kx * 4
                a1s[row : row + 4, 0:16] = w1[kx, ky, kz].astype(F32)
    base = a1s[...]
    t1 = base
    for x in range(1, 4):
        t1 = t1 + pltpu.roll(pltpu.roll(base, 4 * x, 0), 16 * x, 1)
    a1[...] = t1.T[0:64].astype(BF16)

    w2f[...] = jnp.zeros_like(w2f)
    w2f[:, 0:32] = w2[...].reshape(432, 32).astype(F32)
    a2s[...] = jnp.zeros_like(a2s)
    for ky in range(3):
        for kx in range(3):
            a2s[ky * 288 + kx * 48 : ky * 288 + kx * 48 + 48, :] = w2f[(kx * 3 + ky) * 48 : (kx * 3 + ky) * 48 + 48, :]
    base = a2s[...]
    t2 = base
    for x in range(1, 4):
        t2 = t2 + pltpu.roll(pltpu.roll(base, 48 * x, 0), 32 * x, 1)
    a2[...] = t2.T.astype(BF16)
    for ky in range(3):
        for kz in range(3):
            rows = [((kx * 3 + 2 - ky) * 3 + 2 - kz) * 16 for kx in range(3)]
            blocks = [w2f[r : r + 16, :] for r in rows]
            first = blocks[2] + pltpu.roll(blocks[1], 32, 1) + pltpu.roll(blocks[0], 64, 1)
            both = jnp.concatenate([first, pltpu.roll(first, 32, 1)], axis=0)
            a3[:, (ky * 3 + kz) * 128 : (ky * 3 + kz) * 128 + 128] = both.astype(BF16)

    zrow = lax.broadcasted_iota(jnp.int32, (256, 128), 0)
    zcol = lax.broadcasted_iota(jnp.int32, (256, 128), 1)
    halve = jnp.where(lax.div(zrow, 2) == zcol, 0.125, 0.0).astype(BF16)
    zrow = lax.broadcasted_iota(jnp.int32, (128, 256), 0)
    zcol = lax.broadcasted_iota(jnp.int32, (128, 256), 1)
    double = jnp.where(zrow == lax.div(zcol, 2), 1.0, 0.0).astype(BF16)

    acc1[...] = jnp.zeros_like(acc1)
    acc2[...] = jnp.zeros_like(acc2)
    for s in range(2):
        u1[s, 0:80, :] = jnp.zeros((80, 256), BF16)
        u1[s, 1360:1456, :] = jnp.zeros((96, 256), BF16)
        u2[s, 0:288, :] = jnp.zeros((288, 128), BF16)
        u2[s, 2592:2912, :] = jnp.zeros((320, 128), BF16)
        u3[s, 0:384, :] = jnp.zeros((384, 128), BF16)
        u3[s, 3456:3840, :] = jnp.zeros((384, 128), BF16)

    def stage1(s):
        arrive(halos[s], vbuf.at[s, 0], vbuf.at[s, 5])
        planes = vbuf[s].reshape(384, 256).astype(F32)
        for half in range(2):
            vf[half] = planes[:, 128 * half : 128 * half + 128]

        def fill(y, c):
            v = jnp.concatenate([vf[half, pl.ds(y, 24, stride=16), :] for half in range(2)], axis=1)
            before, after = shifts(v)
            rows = jnp.concatenate([before, v, after, jnp.zeros((8, 256), F32)], axis=0)
            u1[s, pl.ds(pl.multiple_of((y + 1) * 80, 16), 80), :] = rows.astype(BF16)
            return c

        lax.fori_loop(0, 16, fill, 0, unroll=4)

        def forward(j, c):
            total = None
            for i in range(2):
                y = 2 * j + i
                pre = dot(a1[...], u1[s, pl.ds(pl.multiple_of(y * 80, 16), 256), :])
                act, sl = act_and_slope(pre)
                slope[s, pl.ds(pl.multiple_of(y * 64, 64), 64), :] = 0.125 * sl
                total = act if total is None else total + act
            pairs = jnp.concatenate([total[0:16] + total[16:32], total[32:48] + total[48:64]], axis=0)
            high, low = split(pairs)
            pooled = (dot(high, halve) + dot(low, halve)).astype(BF16)
            pb[s, j] = pooled.reshape(2, 16, 128)
            mid = pooled.astype(F32)
            before, after = shifts(mid)
            for x in range(2):
                part = slice(16 * x, 16 * x + 16)
                rows = jnp.concatenate([before[part], mid[part], after[part]], axis=0)
                u2[s, pl.ds(pl.multiple_of((j + 1) * 288 + (x + 2) * 48, 16), 48), :] = rows.astype(BF16)
            return c

        lax.fori_loop(0, 8, forward, 0, unroll=4)
        pair = both_ways(2 + s, pb.at[s], ph.at[s, 0], pb.at[s], ph.at[s, 1])
        for c in pair:
            c.start()
        return pair

    def stage2(s, pair):
        for x in range(2):
            cotf[x + 1] = cotb[s, :, x].reshape(256, 128).astype(F32)
        arrive(cot_pairs[s], ch.at[s, 0], ch.at[s, 1])
        for side in range(2):
            cotf[3 * side] = ch[s, side].reshape(256, 128).astype(F32)
        arrive(pair, ph.at[s, 0], ph.at[s, 1])

        def fill(j, c):
            for side in range(2):
                mid = ph[s, side, j].reshape(32, 128).astype(F32)
                before, after = shifts(mid)
                for x in range(2):
                    part = slice(16 * x, 16 * x + 16)
                    rows = jnp.concatenate([before[part], mid[part], after[part]], axis=0)
                    at = pl.multiple_of((j + 1) * 288 + (side * 4 + x) * 48, 16)
                    u2[s, pl.ds(at, 48), :] = rows.astype(BF16)
            return c

        lax.fori_loop(0, 8, fill, 0, unroll=4)

        def forward(j, c):
            pre = dot(a2[...], u2[s, pl.ds(pl.multiple_of(j * 288, 32), 896), :])
            act, sl = act_and_slope(pre)
            for x in range(2):
                actf[pl.ds(x * 8 + j, 32, stride=16), :] = act[32 + 32 * x : 64 + 32 * x]
            got = [cotf[x, pl.ds(j, 32, stride=8), :] for x in range(4)]
            delta = (jnp.concatenate(got, axis=0) * sl).astype(BF16)
            db[s, j] = delta[32:96]
            mid = delta.astype(F32)
            before, after = shifts(mid)
            for kz, rows in enumerate((before, mid, after)):
                u3[s, pl.ds(pl.multiple_of((j + 1) * 384 + kz * 128, 128), 128), :] = rows.astype(BF16)
            return c

        lax.fori_loop(0, 8, forward, 0, unroll=4)
        actb[s] = actf[...].reshape(32, 2, 8, 128).astype(BF16)
        act_copy = pltpu.make_async_copy(actb.at[s], out_act.at[s], local_sem.at[9 + s])
        act_copy.start()
        return act_copy

    def second_grad(s):
        def grad(j, c):
            fields, deltas = [], []
            for i in range(2):
                y = 2 * j + i
                rows = [u2[s, pl.ds(pl.multiple_of((y + ky) * 288 + 48, 16), 192), :] for ky in range(3)]
                fields.append(jnp.concatenate(rows, axis=0))
                deltas.append(db[s, y])
            acc2[:, 0:64] += dot_nt(jnp.concatenate(fields, axis=1), jnp.concatenate(deltas, axis=1))
            return c

        lax.fori_loop(0, 4, grad, 0, unroll=2)

    def stage3(s):
        def backward(j, c):
            back = dot(a3[...], u3[s, pl.ds(pl.multiple_of(j * 384, 128), 1152), :])
            for x in range(2):
                bkf[pl.ds(x * 8 + j, 16, stride=16), :] = back[16 * x : 16 * x + 16]
            high, low = split(back)
            up = dot(high, double) + dot(low, double)
            up = jnp.concatenate([up[0:16], up[0:16], up[16:32], up[16:32]], axis=0)
            fields, deltas = [], []
            for i in range(2):
                y = 2 * j + i
                deltas.append((up * slope[s, pl.ds(pl.multiple_of(y * 64, 64), 64), :]).astype(BF16))
                fields.append(u1[s, pl.ds(pl.multiple_of(y * 80, 16), 256), :])
            acc1[:, 0:64] += dot_nt(jnp.concatenate(fields, axis=1), jnp.concatenate(deltas, axis=1))
            return c

        lax.fori_loop(0, 8, backward, 0, unroll=4)
        bkb[s] = bkf[...].reshape(16, 2, 8, 128).astype(BF16)
        copy = pltpu.make_async_copy(bkb.at[s], out_pg.at[s], local_sem.at[11 + s])
        copy.start()
        return copy

    def exchange(phase, group, index, peer, src, dst):
        def make(d):
            other = lax.rem(index + d, group)
            return pltpu.make_async_remote_copy(
                src_ref=src(other), dst_ref=dst, send_sem=sum_send.at[phase, d], recv_sem=sum_recv.at[phase, d],
                device_id=peer(other), device_id_type=MESH,
            )

        def go(d, c):
            make(d).start()
            return c

        def end(d, c):
            make(d).wait()
            return c

        lax.fori_loop(1, group, go, 0)
        return lambda: lax.fori_loop(1, group, end, 0)

    pooled_pairs = [stage1(0), stage1(1)]
    copies = []
    for s in range(2):
        copies.append(stage2(s, pooled_pairs[s]))
        if s == 0:
            copies.append(stage3(0))
        second_grad(s)

    lanes = lax.broadcasted_iota(jnp.int32, (432, 128), 1)
    g = acc2[...].reshape(3, 192, 128)
    upper = g[:, 48:192].reshape(432, 128)
    f2 = jnp.where(lanes < 32, g[:, 0:144].reshape(432, 128) + pltpu.roll(upper, 96, 1), 0.0)
    packed = f2[0:128]
    rest = [f2[128:144]]
    for ky in range(1, 3):
        packed = packed + pltpu.roll(f2[ky * 144 : ky * 144 + 128], 32 * ky, 1)
        rest.append(f2[ky * 144 + 128 : ky * 144 + 144])
    rest = pltpu.roll(jnp.concatenate(rest, axis=0), 96, 1)
    packed = packed + jnp.concatenate([rest, jnp.zeros((80, 128), F32)], axis=0)
    pack2[...] = packed.reshape(16, 8, 128)

    r1[i1] = pack2[pl.ds(i1 * tp, tp)]
    scattered = exchange(0, g1, i1, peer1, lambda p: pack2.at[pl.ds(p * tp, tp)], r1.at[i1])

    copies.append(stage3(1))

    g = acc1[0:240, :]
    f1 = g
    for x in range(1, 4):
        f1 = f1 + pltpu.roll(pltpu.roll(g, 240 - 4 * x, 0), 128 - 16 * x, 1)
    rows = lax.rem(lax.broadcasted_iota(jnp.int32, (240, 128), 0), 80)
    f1 = jnp.where(lax.broadcasted_iota(jnp.int32, (240, 128), 1) < 16, f1, 0.0)
    f1c = None
    for kz in range(3):
        part = jnp.where((rows >= 24 * kz) & (rows < 24 * kz + 12), f1, 0.0)
        part = pltpu.roll(part, 240 - 12 * kz, 0) if kz else part
        f1c = part if f1c is None else f1c + part
    f1c = f1c.reshape(3, 80, 128)[:, 0:40].reshape(120, 128)
    f1c = jnp.concatenate([f1c, jnp.zeros((8, 128), F32)], axis=0)
    packed = f1c[0:16]
    for k in range(1, 8):
        packed = packed + pltpu.roll(f1c[16 * k : 16 * k + 16], 16 * k, 1)
    p1[i1] = packed
    within = exchange(3, g1, i1, peer1, lambda p: p1.at[i1], p1.at[i1])
    scattered()
    r2[i2] = jnp.sum(r1[...], axis=0)
    crossed = exchange(1, g2, i2, peer2, lambda p: r2.at[i2], r2.at[i2])
    within()
    q1[i2] = jnp.sum(p1[...], axis=0)
    over = exchange(4, g2, i2, peer2, lambda p: q1.at[i2], q1.at[i2])
    crossed()
    res[i1] = jnp.sum(r2[...], axis=0)
    gathered = exchange(2, g1, i1, peer1, lambda p: res.at[i1], res.at[i1])
    over()
    out_s1[...] = jnp.sum(q1[...], axis=0)
    gathered()
    out_s2[...] = res[...].reshape(128, 128)
    for c in copies:
        c.wait()


def finish(
    scales, act, pg, s1, s2, out_act, out_pg, out_g1, out_g2, actv, pgv, sums1, sums2, flat, g1v, g2v, sem
):
    loads = [
        pltpu.make_async_copy(src, dst, sem.at[k])
        for k, (src, dst) in enumerate(((s1, sums1), (s2, sums2), (act, actv), (pg, pgv)))
    ]
    stores = [
        pltpu.make_async_copy(src, dst, sem.at[4 + k])
        for k, (src, dst) in enumerate(((actv, out_act), (pgv, out_pg), (g1v, out_g1), (g2v, out_g2)))
    ]
    for c in loads:
        c.start()
    for k in (2, 3):
        loads[k].wait()
        stores[k - 2].start()
    for c in loads[0:2]:
        c.wait()
    total = sums2[...] * scales[1]
    rest = pltpu.roll(total[0:48], 32, 1)
    for ky in range(3):
        part = pltpu.roll(total, 128 - 32 * ky, 1) if ky else total
        whole = jnp.concatenate([part, rest[ky * 16 : ky * 16 + 16]], axis=0)[:, 0:32]
        for kx in range(3):
            g2v[kx, ky] = whole[kx * 48 : kx * 48 + 48].reshape(3, 16, 32)
    total = sums1[...] * scales[0]
    for k in range(8):
        flat[16 * k : 16 * k + 16, :] = pltpu.roll(total, 128 - 16 * k, 1) if k else total
    for kx in range(3):
        for ky in range(3):
            for kz in range(3):
                row = ky * 40 + kz * 12 + kx * 4
                g1v[kx, ky, kz] = flat[row : row + 4, 0:16]
    for c in stores[2:]:
        c.start()
    for c in stores:
        c.wait()


def solution(mesh):
    sizes = (space_grid(mesh.shape["space"]), mesh.shape["batch"])

    def body(volumes, first_kernel, second_kernel, cotangent):
        cells = math.prod(volumes.shape) // volumes.shape[1] * mesh.size
        scales = (1.0 / math.sqrt(cells), 1.0 / math.sqrt(cells / 8))
        w1 = jnp.transpose(first_kernel, (2, 3, 4, 1, 0))
        w2 = jnp.transpose(second_kernel, (2, 3, 4, 1, 0))
        hbm = pl.BlockSpec(memory_space=pltpu.HBM)
        g1 = sizes[0][0] * sizes[0][2]
        g2 = sizes[0][1] * sizes[1]
        vmem_limit = 60 * 1024 * 1024
        act, pooled_grad, sums1, sums2 = pl.pallas_call(
            functools.partial(kernel, sizes),
            out_shape=(
                jax.ShapeDtypeStruct((2, 32, 2, 8, 128), BF16),
                jax.ShapeDtypeStruct((2, 16, 2, 8, 128), BF16),
                jax.ShapeDtypeStruct((16, 128), F32),
                jax.ShapeDtypeStruct((128, 128), F32),
            ),
            in_specs=[hbm] * 4,
            out_specs=(hbm, hbm, pl.BlockSpec(memory_space=pltpu.VMEM), pl.BlockSpec(memory_space=pltpu.VMEM)),
            scratch_shapes=[
                pltpu.VMEM((2, 6, 4, 16, 256), BF16),
                pltpu.VMEM((2, 384, 128), F32),
                pltpu.VMEM((2, 1456, 256), BF16),
                pltpu.VMEM((2, 1024, 256), F32),
                pltpu.VMEM((2, 8, 2, 16, 128), BF16),
                pltpu.VMEM((2, 2, 8, 2, 16, 128), BF16),
                pltpu.VMEM((2, 2912, 128), BF16),
                pltpu.VMEM((2, 32, 2, 8, 128), BF16),
                pltpu.VMEM((2, 2, 32, 8, 128), BF16),
                pltpu.VMEM((4, 256, 128), F32),
                pltpu.VMEM((512, 128), F32),
                pltpu.VMEM((2, 32, 2, 8, 128), BF16),
                pltpu.VMEM((2, 8, 64, 128), BF16),
                pltpu.VMEM((2, 3840, 128), BF16),
                pltpu.VMEM((256, 128), F32),
                pltpu.VMEM((2, 16, 2, 8, 128), BF16),
                pltpu.VMEM((3, 3, 3, 4, 16), BF16),
                pltpu.VMEM((3, 3, 3, 16, 32), BF16),
                pltpu.VMEM((256, 128), F32),
                pltpu.VMEM((896, 128), F32),
                pltpu.VMEM((432, 128), F32),
                pltpu.VMEM((64, 256), BF16),
                pltpu.VMEM((128, 896), BF16),
                pltpu.VMEM((32, 1152), BF16),
                pltpu.VMEM((256, 128), F32),
                pltpu.VMEM((576, 128), F32),
                pltpu.VMEM((16, 8, 128), F32),
                pltpu.VMEM((g1, 16, 128), F32),
                pltpu.VMEM((g2, 16, 128), F32),
                pltpu.VMEM((g1, 16 // g1, 8, 128), F32),
                pltpu.VMEM((g2, 16 // g1, 8, 128), F32),
                pltpu.VMEM((g1, 16 // g1, 8, 128), F32),
                pltpu.SemaphoreType.DMA((15,)),
                pltpu.SemaphoreType.DMA((6, 2)),
                pltpu.SemaphoreType.DMA((6, 2)),
                pltpu.SemaphoreType.DMA((5, max(g1, g2))),
                pltpu.SemaphoreType.DMA((5, max(g1, g2))),
            ],
            compiler_params=pltpu.CompilerParams(
                collective_id=0, has_side_effects=True, vmem_limit_bytes=vmem_limit
            ),
        )(volumes, w1, w2, cotangent)
        act, pooled_grad, grad1, grad2 = pl.pallas_call(
            functools.partial(finish, scales),
            out_shape=(
                jax.ShapeDtypeStruct((2, 32, 2, 8, 128), BF16),
                jax.ShapeDtypeStruct((2, 16, 2, 8, 128), BF16),
                jax.ShapeDtypeStruct((3, 3, 3, 4, 16), F32),
                jax.ShapeDtypeStruct((3, 3, 3, 16, 32), F32),
            ),
            in_specs=[hbm] * 4,
            out_specs=(hbm,) * 4,
            scratch_shapes=[
                pltpu.VMEM((2, 32, 2, 8, 128), BF16),
                pltpu.VMEM((2, 16, 2, 8, 128), BF16),
                pltpu.VMEM((16, 128), F32),
                pltpu.VMEM((128, 128), F32),
                pltpu.VMEM((128, 128), F32),
                pltpu.VMEM((3, 3, 3, 4, 16), F32),
                pltpu.VMEM((3, 3, 3, 16, 32), F32),
                pltpu.SemaphoreType.DMA((8,)),
            ],
            compiler_params=pltpu.CompilerParams(vmem_limit_bytes=vmem_limit),
        )(act, pooled_grad, sums1, sums2)
        return (
            act,
            pooled_grad,
            jnp.transpose(grad1, (4, 3, 0, 1, 2)),
            jnp.transpose(grad2, (4, 3, 0, 1, 2)),
        )

    return jax.shard_map(
        body,
        mesh=mesh,
        in_specs=(
            P("batch", None, "space", None, None),
            P(),
            P(),
            P("batch", None, "space", None, None),
        ),
        out_specs=(
            P("batch", None, "space", None, None),
            P("batch", None, "space", None, None),
            P(),
            P(),
        ),
        check_vma=False,
    )
```

time: 64.5 us -> 55.7 us (0.86)
  local copies, waits for them, and re-layouts: 6.2 us -> 0 us
  Pallas kernels: 57.4 us -> 55 us
    unnamed x12 -> x0, local copies, waits for them, and re-layouts: 6.2 us -> none
    pallas_call x1 -> x2, Pallas kernels: 57.4 us -> 55 us  [the longest x1 53 us: body(): pl.pallas_call(functools.partial(kernel, sizes), out_shape=(jax.ShapeDtyp...]
where the time goes in v1:
time: 55.7 us; the launch traced here: 55.6 us
  Pallas kernels  55 us (99%)
  between operations  0.64 us (1%)
    pallas_call x1, Pallas kernels, body(): pl.pallas_call(functools.partial(kernel, sizes), out_shape=(jax.ShapeDtyp...  53 us
    pallas_call x1, Pallas kernels, body(): pl.pallas_call(functools.partial(finish, scales), out_shape=(jax.ShapeDty...  1.92 us

profile of v1, /device:TPU:1, one launch (start us, length us, event | category | flops | bytes accessed | tf_op | source)
XLA Modules:
  0.0 55.6 jit_solution(14212537494793886391)
XLA Ops:
  0.6 53.0 %shard_map.75 = (bf16[2,32,2,8,128]{4,3,2,1,0:T(8,128)(2,1)}, bf16[2,16,2,8,128]{4,3,2,1,0:T(8,128)(2,1)}, f32[16,128]{1,0:T(8,128)}, f32[128,128]{1,0:T(8,128)}) custom-call(bf16[2,4,4,16,256]{4,3,2,1,0:T(8,128)(2,1)} %vol.1, bf16[3,3,3,4,16]{4,3,2,1,0:T(4,128)(2,1)} %bitcast.5, bf16[3,3,3,16,32]{4,3,2,1,0:T(8,128)(2,1)} %bitcast.4, ...), custom_call_target="tpu_custom_call" | custom-call | tf_op jit(solution)/shard_map/pallas_call | solution.py:434
  53.7 1.9 %shard_map.76 = (bf16[2,32,2,8,128]{4,3,2,1,0:T(8,128)(2,1)}, bf16[2,16,2,8,128]{4,3,2,1,0:T(8,128)(2,1)}, f32[3,3,3,4,16]{4,3,2,1,0:T(4,128)}, f32[3,3,3,16,32]{4,3,2,1,0:T(8,128)}) custom-call(bf16[2,32,2,8,128]{4,3,2,1,0:T(8,128)(2,1)} %get-tuple-element.12.act, bf16[2,16,2,8,128]{4,3,2,1,0:T(8,128)(2,1)} %get-tuple-element.13.pg, ...), custom_call_target="tpu_custom_call" | custom-call | tf_op jit(solution)/shard_map/pallas_call | solution.py:487

commit v2 on v1

--- a/solution.py
+++ b/solution.py
@@ -36,9 +36,20 @@
     return before, after
 
 
-def split(v):
-    high = v.astype(BF16)
-    return high, (v - high.astype(F32)).astype(BF16)
+def pair_sums(v):
+    first, second = v[:, 0:128], v[:, 128:256]
+    lanes = lax.broadcasted_iota(jnp.int32, first.shape, 1)
+    mixed = jnp.where(
+        (lanes & 1) == 0, first + pltpu.roll(first, 127, 1), second + pltpu.roll(second, 1, 1)
+    )
+    source = jnp.where(lanes < 64, 2 * lanes, 2 * lanes - 127)
+    return jnp.take_along_axis(mixed, source, axis=1)
+
+
+def doubled(v):
+    lanes = lax.broadcasted_iota(jnp.int32, v.shape, 1)
+    half = lanes >> 1
+    return [jnp.take_along_axis(v, half, axis=1), jnp.take_along_axis(v, half + 64, axis=1)]
 
 
 def act_and_slope(z):
@@ -49,7 +60,7 @@
 
 def kernel(
     sizes, vol, w1_hbm, w2_hbm, cot, out_act, out_pg, out_s1, out_s2,
-    vbuf, vf, u1, slope, pb, ph, u2, cotb, ch, cotf, actf, actb, db, u3, bkf, bkb,
+    vbuf, vf, u1, slope, pb, ph, u2, cotb, ch, cotf, actf, actb, db, fd, u3, bkf, bkb,
     w1, w2, a1s, a2s, w2f, a1, a2, a3, acc1, acc2, pack2, p1, q1, r1, r2, res,
     local_sem, halo_send, halo_recv, sum_send, sum_recv,
 ):
@@ -164,61 +175,46 @@
             blocks = [w2f[r : r + 16, :] for r in rows]
             first = blocks[2] + pltpu.roll(blocks[1], 32, 1) + pltpu.roll(blocks[0], 64, 1)
             both = jnp.concatenate([first, pltpu.roll(first, 32, 1)], axis=0)
-            a3[:, (ky * 3 + kz) * 128 : (ky * 3 + kz) * 128 + 128] = both.astype(BF16)
-
-    zrow = lax.broadcasted_iota(jnp.int32, (256, 128), 0)
-    zcol = lax.broadcasted_iota(jnp.int32, (256, 128), 1)
-    halve = jnp.where(lax.div(zrow, 2) == zcol, 0.125, 0.0).astype(BF16)
-    zrow = lax.broadcasted_iota(jnp.int32, (128, 256), 0)
-    zcol = lax.broadcasted_iota(jnp.int32, (128, 256), 1)
-    double = jnp.where(zrow == lax.div(zcol, 2), 1.0, 0.0).astype(BF16)
-
-    acc1[...] = jnp.zeros_like(acc1)
-    acc2[...] = jnp.zeros_like(acc2)
+            a3[32 * ky : 32 * ky + 32, kz * 128 : kz * 128 + 128] = both.astype(BF16)
+
     for s in range(2):
         u1[s, 0:80, :] = jnp.zeros((80, 256), BF16)
         u1[s, 1360:1456, :] = jnp.zeros((96, 256), BF16)
         u2[s, 0:288, :] = jnp.zeros((288, 128), BF16)
         u2[s, 2592:2912, :] = jnp.zeros((320, 128), BF16)
-        u3[s, 0:384, :] = jnp.zeros((384, 128), BF16)
-        u3[s, 3456:3840, :] = jnp.zeros((384, 128), BF16)
+        for y in (0, 9):
+            db[s, y] = jnp.zeros((64, 128), BF16)
+        for y in (0, 17):
+            fd[s, y] = jnp.zeros((64, 256), BF16)
 
     def stage1(s):
         arrive(halos[s], vbuf.at[s, 0], vbuf.at[s, 5])
         planes = vbuf[s].reshape(384, 256).astype(F32)
         for half in range(2):
             vf[half] = planes[:, 128 * half : 128 * half + 128]
-
-        def fill(y, c):
+        for y in range(16):
             v = jnp.concatenate([vf[half, pl.ds(y, 24, stride=16), :] for half in range(2)], axis=1)
             before, after = shifts(v)
             rows = jnp.concatenate([before, v, after, jnp.zeros((8, 256), F32)], axis=0)
-            u1[s, pl.ds(pl.multiple_of((y + 1) * 80, 16), 80), :] = rows.astype(BF16)
-            return c
-
-        lax.fori_loop(0, 16, fill, 0, unroll=4)
-
-        def forward(j, c):
+            u1[s, (y + 1) * 80 : (y + 2) * 80, :] = rows.astype(BF16)
+        for j in range(8):
             total = None
             for i in range(2):
                 y = 2 * j + i
-                pre = dot(a1[...], u1[s, pl.ds(pl.multiple_of(y * 80, 16), 256), :])
+                pre = dot(a1[...], u1[s, y * 80 : y * 80 + 256, :])
                 act, sl = act_and_slope(pre)
-                slope[s, pl.ds(pl.multiple_of(y * 64, 64), 64), :] = 0.125 * sl
+                slope[s, y * 64 : y * 64 + 64, :] = 0.125 * sl
                 total = act if total is None else total + act
             pairs = jnp.concatenate([total[0:16] + total[16:32], total[32:48] + total[48:64]], axis=0)
-            high, low = split(pairs)
-            pooled = (dot(high, halve) + dot(low, halve)).astype(BF16)
+            pooled = (0.125 * pair_sums(pairs)).astype(BF16)
             pb[s, j] = pooled.reshape(2, 16, 128)
             mid = pooled.astype(F32)
             before, after = shifts(mid)
             for x in range(2):
                 part = slice(16 * x, 16 * x + 16)
                 rows = jnp.concatenate([before[part], mid[part], after[part]], axis=0)
-                u2[s, pl.ds(pl.multiple_of((j + 1) * 288 + (x + 2) * 48, 16), 48), :] = rows.astype(BF16)
-            return c
-
-        lax.fori_loop(0, 8, forward, 0, unroll=4)
+                at = (j + 1) * 288 + (x + 2) * 48
+                u2[s, at : at + 48, :] = rows.astype(BF16)
         pair = both_ways(2 + s, pb.at[s], ph.at[s, 0], pb.at[s], ph.at[s, 1])
         for c in pair:
             c.start()
@@ -231,74 +227,69 @@
         for side in range(2):
             cotf[3 * side] = ch[s, side].reshape(256, 128).astype(F32)
         arrive(pair, ph.at[s, 0], ph.at[s, 1])
-
-        def fill(j, c):
+        for j in range(8):
             for side in range(2):
                 mid = ph[s, side, j].reshape(32, 128).astype(F32)
                 before, after = shifts(mid)
                 for x in range(2):
                     part = slice(16 * x, 16 * x + 16)
                     rows = jnp.concatenate([before[part], mid[part], after[part]], axis=0)
-                    at = pl.multiple_of((j + 1) * 288 + (side * 4 + x) * 48, 16)
-                    u2[s, pl.ds(at, 48), :] = rows.astype(BF16)
-            return c
-
-        lax.fori_loop(0, 8, fill, 0, unroll=4)
-
-        def forward(j, c):
-            pre = dot(a2[...], u2[s, pl.ds(pl.multiple_of(j * 288, 32), 896), :])
+                    at = (j + 1) * 288 + (side * 4 + x) * 48
+                    u2[s, at : at + 48, :] = rows.astype(BF16)
+        for j in range(8):
+            pre = dot(a2[...], u2[s, j * 288 : j * 288 + 896, :])
             act, sl = act_and_slope(pre)
             for x in range(2):
                 actf[pl.ds(x * 8 + j, 32, stride=16), :] = act[32 + 32 * x : 64 + 32 * x]
             got = [cotf[x, pl.ds(j, 32, stride=8), :] for x in range(4)]
             delta = (jnp.concatenate(got, axis=0) * sl).astype(BF16)
-            db[s, j] = delta[32:96]
+            db[s, j + 1] = delta[32:96]
             mid = delta.astype(F32)
             before, after = shifts(mid)
             for kz, rows in enumerate((before, mid, after)):
-                u3[s, pl.ds(pl.multiple_of((j + 1) * 384 + kz * 128, 128), 128), :] = rows.astype(BF16)
-            return c
-
-        lax.fori_loop(0, 8, forward, 0, unroll=4)
+                u3[s, j * 384 + kz * 128 : j * 384 + kz * 128 + 128, :] = rows.astype(BF16)
         actb[s] = actf[...].reshape(32, 2, 8, 128).astype(BF16)
         act_copy = pltpu.make_async_copy(actb.at[s], out_act.at[s], local_sem.at[9 + s])
         act_copy.start()
         return act_copy
 
     def second_grad(s):
-        def grad(j, c):
-            fields, deltas = [], []
-            for i in range(2):
-                y = 2 * j + i
-                rows = [u2[s, pl.ds(pl.multiple_of((y + ky) * 288 + 48, 16), 192), :] for ky in range(3)]
-                fields.append(jnp.concatenate(rows, axis=0))
-                deltas.append(db[s, y])
-            acc2[:, 0:64] += dot_nt(jnp.concatenate(fields, axis=1), jnp.concatenate(deltas, axis=1))
-            return c
-
-        lax.fori_loop(0, 4, grad, 0, unroll=2)
+        fields = [u2[s, (y + 1) * 288 + 48 : (y + 1) * 288 + 240, :] for y in range(8)]
+        deltas = [db[s, y : y + 3].reshape(192, 128) for y in range(8)]
+        return dot_nt(jnp.concatenate(fields, axis=1), jnp.concatenate(deltas, axis=1))
 
     def stage3(s):
-        def backward(j, c):
-            back = dot(a3[...], u3[s, pl.ds(pl.multiple_of(j * 384, 128), 1152), :])
+        parts = []
+        for j in range(4):
+            both = jnp.concatenate([u3[s, (2 * j + i) * 384 : (2 * j + i) * 384 + 384, :] for i in range(2)], axis=1)
+            part = dot(a3[...], both)
+            parts += [part[:, 0:128], part[:, 128:256]]
+        for j in range(8):
+            back = parts[j][32:64]
+            if j > 0:
+                back = back + parts[j - 1][0:32]
+            if j < 7:
+                back = back + parts[j + 1][64:96]
             for x in range(2):
                 bkf[pl.ds(x * 8 + j, 16, stride=16), :] = back[16 * x : 16 * x + 16]
-            high, low = split(back)
-            up = dot(high, double) + dot(low, double)
+            up = jnp.concatenate(doubled(back), axis=1)
             up = jnp.concatenate([up[0:16], up[0:16], up[16:32], up[16:32]], axis=0)
-            fields, deltas = [], []
-            for i in range(2):
-                y = 2 * j + i
-                deltas.append((up * slope[s, pl.ds(pl.multiple_of(y * 64, 64), 64), :]).astype(BF16))
-                fields.append(u1[s, pl.ds(pl.multiple_of(y * 80, 16), 256), :])
-            acc1[:, 0:64] += dot_nt(jnp.concatenate(fields, axis=1), jnp.concatenate(deltas, axis=1))
-            return c
-
-        lax.fori_loop(0, 8, backward, 0, unroll=4)
+            for y in (2 * j, 2 * j + 1):
+                fd[s, y + 1] = (up * slope[s, y * 64 : y * 64 + 64, :]).astype(BF16)
         bkb[s] = bkf[...].reshape(16, 2, 8, 128).astype(BF16)
         copy = pltpu.make_async_copy(bkb.at[s], out_pg.at[s], local_sem.at[11 + s])
         copy.start()
         return copy
+
+    def first_grad(s):
+        total = None
+        for k in range(4):
+            ys = range(4 * k, 4 * k + 4)
+            fields = [u1[s, (y + 1) * 80 : (y + 2) * 80, :] for y in ys]
+            deltas = [fd[s, y : y + 3].reshape(192, 256) for y in ys]
+            part = dot_nt(jnp.concatenate(fields, axis=1), jnp.concatenate(deltas, axis=1))
+            total = part if total is None else total + part
+        return total
 
     def exchange(phase, group, index, peer, src, dst):
         def make(d):
@@ -320,47 +311,60 @@
         return lambda: lax.fori_loop(1, group, end, 0)
 
     pooled_pairs = [stage1(0), stage1(1)]
-    copies = []
-    for s in range(2):
-        copies.append(stage2(s, pooled_pairs[s]))
-        if s == 0:
-            copies.append(stage3(0))
-        second_grad(s)
-
-    lanes = lax.broadcasted_iota(jnp.int32, (432, 128), 1)
-    g = acc2[...].reshape(3, 192, 128)
-    upper = g[:, 48:192].reshape(432, 128)
-    f2 = jnp.where(lanes < 32, g[:, 0:144].reshape(432, 128) + pltpu.roll(upper, 96, 1), 0.0)
-    packed = f2[0:128]
-    rest = [f2[128:144]]
-    for ky in range(1, 3):
-        packed = packed + pltpu.roll(f2[ky * 144 : ky * 144 + 128], 32 * ky, 1)
-        rest.append(f2[ky * 144 + 128 : ky * 144 + 144])
-    rest = pltpu.roll(jnp.concatenate(rest, axis=0), 96, 1)
-    packed = packed + jnp.concatenate([rest, jnp.zeros((80, 128), F32)], axis=0)
-    pack2[...] = packed.reshape(16, 8, 128)
+    copies = [stage2(0, pooled_pairs[0]), stage3(0)]
+    acc1[:, 0:192] = first_grad(0)
+    acc2[:, 0:192] = second_grad(0)
+    copies.append(stage2(1, pooled_pairs[1]))
+    acc2[:, 0:192] += second_grad(1)
+
+    lanes = lax.broadcasted_iota(jnp.int32, (144, 128), 1)
+    f2 = None
+    for f in range(3):
+        ky = 2 - f
+        tile = acc2[:, 128 * (f // 2) : 128 * (f // 2) + 128]
+        move = 32 * ky - 64 * (f % 2)
+        part = pltpu.roll(tile[0:144], move % 128, 1) if move % 128 else tile[0:144]
+        part = part + pltpu.roll(tile[48:192], (move - 32) % 128, 1)
+        part = jnp.where((lanes >= 32 * ky) & (lanes < 32 * ky + 32), part, 0.0)
+        f2 = part if f2 is None else f2 + part
+    rest = []
+    for ky in range(3):
+        part = pltpu.roll(f2[128:144], 96 - 32 * ky, 1)
+        rest.append(jnp.where(lanes[0:16] >= 96, part, 0.0))
+    rest = jnp.concatenate(rest + [jnp.zeros((80, 128), F32)], axis=0)
+    pack2[...] = (f2[0:128] + rest).reshape(16, 8, 128)
 
     r1[i1] = pack2[pl.ds(i1 * tp, tp)]
     scattered = exchange(0, g1, i1, peer1, lambda p: pack2.at[pl.ds(p * tp, tp)], r1.at[i1])
 
     copies.append(stage3(1))
-
-    g = acc1[0:240, :]
-    f1 = g
-    for x in range(1, 4):
-        f1 = f1 + pltpu.roll(pltpu.roll(g, 240 - 4 * x, 0), 128 - 16 * x, 1)
-    rows = lax.rem(lax.broadcasted_iota(jnp.int32, (240, 128), 0), 80)
-    f1 = jnp.where(lax.broadcasted_iota(jnp.int32, (240, 128), 1) < 16, f1, 0.0)
-    f1c = None
-    for kz in range(3):
-        part = jnp.where((rows >= 24 * kz) & (rows < 24 * kz + 12), f1, 0.0)
-        part = pltpu.roll(part, 240 - 12 * kz, 0) if kz else part
-        f1c = part if f1c is None else f1c + part
-    f1c = f1c.reshape(3, 80, 128)[:, 0:40].reshape(120, 128)
-    f1c = jnp.concatenate([f1c, jnp.zeros((8, 128), F32)], axis=0)
-    packed = f1c[0:16]
-    for k in range(1, 8):
-        packed = packed + pltpu.roll(f1c[16 * k : 16 * k + 16], 16 * k, 1)
+    acc1[:, 0:192] += first_grad(1)
+
+    rows = lax.broadcasted_iota(jnp.int32, (80, 128), 0)
+    lanes = lax.broadcasted_iota(jnp.int32, (80, 128), 1)
+    folded = []
+    for half in range(2):
+        g = acc1[:, 128 * half : 128 * half + 128]
+        f1 = g
+        for x in range(1, 4):
+            f1 = f1 + pltpu.roll(pltpu.roll(g, 80 - 4 * x, 0), 128 - 16 * x, 1)
+        f1 = jnp.where((lanes & 63) < 16, f1, 0.0)
+        f1c = None
+        for kz in range(3):
+            part = jnp.where((rows >= 24 * kz) & (rows < 24 * kz + 12), f1, 0.0)
+            part = pltpu.roll(part, 80 - 12 * kz, 0) if kz else part
+            f1c = part if f1c is None else f1c + part
+        folded.append(f1c[0:40])
+    packed = [None, None]
+    for f in range(3):
+        for r in range(5):
+            k = f * 5 + r
+            part = folded[f // 2][8 * r : 8 * r + 8]
+            part = jnp.where((lanes[0:8] >> 6) == f % 2, part, 0.0)
+            move = (16 * (k // 2) - 64 * (f % 2)) % 128
+            part = pltpu.roll(part, move, 1) if move else part
+            packed[k % 2] = part if packed[k % 2] is None else packed[k % 2] + part
+    packed = jnp.concatenate(packed, axis=0)
     p1[i1] = packed
     within = exchange(3, g1, i1, peer1, lambda p: p1.at[i1], p1.at[i1])
     scattered()
@@ -406,12 +410,13 @@
         for kx in range(3):
             g2v[kx, ky] = whole[kx * 48 : kx * 48 + 48].reshape(3, 16, 32)
     total = sums1[...] * scales[0]
-    for k in range(8):
-        flat[16 * k : 16 * k + 16, :] = pltpu.roll(total, 128 - 16 * k, 1) if k else total
+    for k in range(15):
+        part = total[8 * (k % 2) : 8 * (k % 2) + 8]
+        flat[8 * k : 8 * k + 8, :] = pltpu.roll(part, 128 - 16 * (k // 2), 1) if k > 1 else part
     for kx in range(3):
         for ky in range(3):
             for kz in range(3):
-                row = ky * 40 + kz * 12 + kx * 4
+                row = (2 - ky) * 40 + kz * 12 + kx * 4
                 g1v[kx, ky, kz] = flat[row : row + 4, 0:16]
     for c in stores[2:]:
         c.start()
@@ -454,8 +459,9 @@
                 pltpu.VMEM((4, 256, 128), F32),
                 pltpu.VMEM((512, 128), F32),
                 pltpu.VMEM((2, 32, 2, 8, 128), BF16),
-                pltpu.VMEM((2, 8, 64, 128), BF16),
-                pltpu.VMEM((2, 3840, 128), BF16),
+                pltpu.VMEM((2, 10, 64, 128), BF16),
+                pltpu.VMEM((2, 18, 64, 256), BF16),
+                pltpu.VMEM((2, 3072, 128), BF16),
                 pltpu.VMEM((256, 128), F32),
                 pltpu.VMEM((2, 16, 2, 8, 128), BF16),
                 pltpu.VMEM((3, 3, 3, 4, 16), BF16),
@@ -465,9 +471,9 @@
                 pltpu.VMEM((432, 128), F32),
                 pltpu.VMEM((64, 256), BF16),
                 pltpu.VMEM((128, 896), BF16),
-                pltpu.VMEM((32, 1152), BF16),
-                pltpu.VMEM((256, 128), F32),
-                pltpu.VMEM((576, 128), F32),
+                pltpu.VMEM((96, 384), BF16),
+                pltpu.VMEM((80, 256), F32),
+                pltpu.VMEM((192, 256), F32),
                 pltpu.VMEM((16, 8, 128), F32),
                 pltpu.VMEM((g1, 16, 128), F32),
                 pltpu.VMEM((g2, 16, 128), F32),

time: 55.7 us -> 50.8 us (0.912)
  Pallas kernels: 55 us -> 50 us
    pallas_call x1, Pallas kernels: 53 us -> 48.1 us  [body(): pl.pallas_call(functools.partial(kernel, sizes), out_shape=(jax.ShapeDtyp...]
where the time goes in v2:
time: 50.8 us; the launch traced here: 50.7 us
  Pallas kernels  50 us (98%)
  between operations  0.64 us (1%)
    pallas_call x1, Pallas kernels, body(): pl.pallas_call(functools.partial(kernel, sizes), out_shape=(jax.ShapeDtyp...  48.1 us
    pallas_call x1, Pallas kernels, body(): pl.pallas_call(functools.partial(finish, scales), out_shape=(jax.ShapeDty...  1.93 us

profile of v2, /device:TPU:1, one launch (start us, length us, event | category | flops | bytes accessed | tf_op | source)
XLA Modules:
  0.0 50.7 jit_solution(8485359162156125025)
XLA Ops:
  0.6 48.1 %shard_map.75 = (bf16[2,32,2,8,128]{4,3,2,1,0:T(8,128)(2,1)}, bf16[2,16,2,8,128]{4,3,2,1,0:T(8,128)(2,1)}, f32[16,128]{1,0:T(8,128)}, f32[128,128]{1,0:T(8,128)}) custom-call(bf16[2,4,4,16,256]{4,3,2,1,0:T(8,128)(2,1)} %vol.1, bf16[3,3,3,4,16]{4,3,2,1,0:T(4,128)(2,1)} %bitcast.5, bf16[3,3,3,16,32]{4,3,2,1,0:T(8,128)(2,1)} %bitcast.4, ...), custom_call_target="tpu_custom_call" | custom-call | tf_op jit(solution)/shard_map/pallas_call | solution.py:439
  48.7 1.9 %shard_map.76 = (bf16[2,32,2,8,128]{4,3,2,1,0:T(8,128)(2,1)}, bf16[2,16,2,8,128]{4,3,2,1,0:T(8,128)(2,1)}, f32[3,3,3,4,16]{4,3,2,1,0:T(4,128)}, f32[3,3,3,16,32]{4,3,2,1,0:T(8,128)}) custom-call(bf16[2,32,2,8,128]{4,3,2,1,0:T(8,128)(2,1)} %get-tuple-element.12.act, bf16[2,16,2,8,128]{4,3,2,1,0:T(8,128)(2,1)} %get-tuple-element.13.pg, ...), custom_call_target="tpu_custom_call" | custom-call | tf_op jit(solution)/shard_map/pallas_call | solution.py:493

commit v3 on v2

--- a/solution.py
+++ b/solution.py
@@ -60,8 +60,8 @@
 
 def kernel(
     sizes, vol, w1_hbm, w2_hbm, cot, out_act, out_pg, out_s1, out_s2,
-    vbuf, vf, u1, slope, pb, ph, u2, cotb, ch, cotf, actf, actb, db, fd, u3, bkf, bkb,
-    w1, w2, a1s, a2s, w2f, a1, a2, a3, acc1, acc2, pack2, p1, q1, r1, r2, res,
+    vbuf, vf, u1, slope, pb, ph, u2, cotb, cotf, actf, db, fd, u3, bko, kb, kh, bkf,
+    w1, w2, a1s, a2s, w2f, a1, a2, a3, acc1, acc2, pack2, p1, pairs, q1, r1, r2, res,
     local_sem, halo_send, halo_recv, sum_send, sum_recv,
 ):
     (nx, nzh, ny), nb = sizes
@@ -74,6 +74,9 @@
     yi = lax.rem(sp, ny)
     i1 = xi * ny + yi
     i2 = zi * nb + bt
+    core = lax.rem(bt, 2)
+    zlow = lax.div(bt, 2)
+    iz = zi * (nb // 2) + zlow
     right = lax.rem(sp + 1, n_space)
     left = lax.rem(sp + n_space - 1, n_space)
 
@@ -82,6 +85,13 @@
 
     def peer2(p):
         return (xi * (nzh * ny) + lax.div(p, nb) * ny + yi, lax.rem(p, nb))
+
+    def peerz(p):
+        low = nb // 2
+        return (xi * (nzh * ny) + lax.div(p, low) * ny + yi, lax.rem(p, low) * 2 + core)
+
+    def peerc(p):
+        return (sp, zlow * 2 + p)
 
     barrier = pltpu.get_barrier_semaphore()
     for side in (left, right):
@@ -103,8 +113,8 @@
         for x in range(4):
             own.append(pltpu.make_async_copy(vol.at[s, :, x], vbuf.at[s, x + 1], local_sem.at[s * 4 + x]))
     own.append(pltpu.make_async_copy(cot, cotb, local_sem.at[8]))
-    own.append(pltpu.make_async_copy(w1_hbm, w1, local_sem.at[13]))
-    own.append(pltpu.make_async_copy(w2_hbm, w2, local_sem.at[14]))
+    own.append(pltpu.make_async_copy(w1_hbm, w1, local_sem.at[9]))
+    own.append(pltpu.make_async_copy(w2_hbm, w2, local_sem.at[10]))
     for c in own:
         c.start()
     for c in own[0:8]:
@@ -129,10 +139,6 @@
             c.start()
     for c in own[8:]:
         c.wait()
-    cot_pairs = [both_ways(4 + s, cotb.at[s, :, 1], ch.at[s, 0], cotb.at[s, :, 0], ch.at[s, 1]) for s in range(2)]
-    for pair in cot_pairs:
-        for c in pair:
-            c.start()
 
     def arrive(pair, low, high):
         for c in pair:
@@ -163,25 +169,24 @@
     a2s[...] = jnp.zeros_like(a2s)
     for ky in range(3):
         for kx in range(3):
-            a2s[ky * 288 + kx * 48 : ky * 288 + kx * 48 + 48, :] = w2f[(kx * 3 + ky) * 48 : (kx * 3 + ky) * 48 + 48, :]
-    base = a2s[...]
-    t2 = base
-    for x in range(1, 4):
-        t2 = t2 + pltpu.roll(pltpu.roll(base, 48 * x, 0), 32 * x, 1)
-    a2[...] = t2.T.astype(BF16)
+            a2s[ky, kx * 48 : kx * 48 + 48, :] = w2f[(kx * 3 + ky) * 48 : (kx * 3 + ky) * 48 + 48, :]
+        base = a2s[ky]
+        both = (base + pltpu.roll(pltpu.roll(base, 48, 0), 32, 1)).T[0:64, 0:192].astype(BF16)
+        a2[64 * ky : 64 * ky + 64, :] = both
     for ky in range(3):
+        pieces = []
         for kz in range(3):
             rows = [((kx * 3 + 2 - ky) * 3 + 2 - kz) * 16 for kx in range(3)]
-            blocks = [w2f[r : r + 16, :] for r in rows]
-            first = blocks[2] + pltpu.roll(blocks[1], 32, 1) + pltpu.roll(blocks[0], 64, 1)
-            both = jnp.concatenate([first, pltpu.roll(first, 32, 1)], axis=0)
-            a3[32 * ky : 32 * ky + 32, kz * 128 : kz * 128 + 128] = both.astype(BF16)
+            zero = jnp.zeros((16, 128), F32)
+            kept = [w2f[r : r + 16, :] for r in rows] + [zero]
+            both = jnp.concatenate(kept, axis=0) + pltpu.roll(jnp.concatenate([zero] + kept[0:3], axis=0), 32, 1)
+            pieces.append(both)
+        a3[64 * ky : 64 * ky + 64, 0:128] = (pieces[0] + pltpu.roll(pieces[1], 64, 1)).astype(BF16)
+        a3[64 * ky : 64 * ky + 64, 128:192] = pieces[2][:, 0:64].astype(BF16)
 
     for s in range(2):
         u1[s, 0:80, :] = jnp.zeros((80, 256), BF16)
         u1[s, 1360:1456, :] = jnp.zeros((96, 256), BF16)
-        u2[s, 0:288, :] = jnp.zeros((288, 128), BF16)
-        u2[s, 2592:2912, :] = jnp.zeros((320, 128), BF16)
         for y in (0, 9):
             db[s, y] = jnp.zeros((64, 128), BF16)
         for y in (0, 17):
@@ -207,79 +212,85 @@
                 total = act if total is None else total + act
             pairs = jnp.concatenate([total[0:16] + total[16:32], total[32:48] + total[48:64]], axis=0)
             pooled = (0.125 * pair_sums(pairs)).astype(BF16)
-            pb[s, j] = pooled.reshape(2, 16, 128)
+            for x in range(2):
+                pb[s, x, j] = pooled[16 * x : 16 * x + 16]
             mid = pooled.astype(F32)
             before, after = shifts(mid)
             for x in range(2):
                 part = slice(16 * x, 16 * x + 16)
                 rows = jnp.concatenate([before[part], mid[part], after[part]], axis=0)
-                at = (j + 1) * 288 + (x + 2) * 48
+                at = j * 192 + (x + 1) * 48
                 u2[s, at : at + 48, :] = rows.astype(BF16)
-        pair = both_ways(2 + s, pb.at[s], ph.at[s, 0], pb.at[s], ph.at[s, 1])
-        for c in pair:
+        near = both_ways(2 + s, pb.at[s, 1], ph.at[s, 0], pb.at[s, 0], ph.at[s, 1])
+        for c in near:
             c.start()
-        return pair
-
-    def stage2(s, pair):
+        return near
+
+    def convolved(matrix, field, count):
+        parts = []
+        for j in range(4):
+            part = dot(matrix, jnp.concatenate([field[2 * j], field[2 * j + 1]], axis=1))
+            parts += [part[:, 0:128], part[:, 128:256]]
+        out = []
+        for j in range(8):
+            pre = parts[j][count : 2 * count]
+            if j > 0:
+                pre = pre + parts[j - 1][0:count]
+            if j < 7:
+                pre = pre + parts[j + 1][2 * count : 3 * count]
+            out.append(pre)
+        return out
+
+    def second_layer(s, near):
         for x in range(2):
-            cotf[x + 1] = cotb[s, :, x].reshape(256, 128).astype(F32)
-        arrive(cot_pairs[s], ch.at[s, 0], ch.at[s, 1])
-        for side in range(2):
-            cotf[3 * side] = ch[s, side].reshape(256, 128).astype(F32)
-        arrive(pair, ph.at[s, 0], ph.at[s, 1])
+            cotf[x] = cotb[s, :, x].reshape(256, 128).astype(F32)
+        arrive(near, ph.at[s, 0], ph.at[s, 1])
         for j in range(8):
+            mid = jnp.concatenate([ph[s, 0, j], ph[s, 1, j]], axis=0).astype(F32)
+            before, after = shifts(mid)
             for side in range(2):
-                mid = ph[s, side, j].reshape(32, 128).astype(F32)
-                before, after = shifts(mid)
-                for x in range(2):
-                    part = slice(16 * x, 16 * x + 16)
-                    rows = jnp.concatenate([before[part], mid[part], after[part]], axis=0)
-                    at = (j + 1) * 288 + (side * 4 + x) * 48
-                    u2[s, at : at + 48, :] = rows.astype(BF16)
-        for j in range(8):
-            pre = dot(a2[...], u2[s, j * 288 : j * 288 + 896, :])
+                part = slice(16 * side, 16 * side + 16)
+                rows = jnp.concatenate([before[part], mid[part], after[part]], axis=0)
+                u2[s, j * 192 + side * 144 : j * 192 + side * 144 + 48, :] = rows.astype(BF16)
+        field = [u2[s, j * 192 : j * 192 + 192, :] for j in range(8)]
+        for j, pre in enumerate(convolved(a2[...], field, 64)):
             act, sl = act_and_slope(pre)
             for x in range(2):
-                actf[pl.ds(x * 8 + j, 32, stride=16), :] = act[32 + 32 * x : 64 + 32 * x]
-            got = [cotf[x, pl.ds(j, 32, stride=8), :] for x in range(4)]
+                actf[pl.ds(x * 8 + j, 32, stride=16), :] = act[32 * x : 32 * x + 32]
+            got = [cotf[x, pl.ds(j, 32, stride=8), :] for x in range(2)]
             delta = (jnp.concatenate(got, axis=0) * sl).astype(BF16)
-            db[s, j + 1] = delta[32:96]
+            db[s, j + 1] = delta
             mid = delta.astype(F32)
             before, after = shifts(mid)
             for kz, rows in enumerate((before, mid, after)):
-                u3[s, j * 384 + kz * 128 : j * 384 + kz * 128 + 128, :] = rows.astype(BF16)
-        actb[s] = actf[...].reshape(32, 2, 8, 128).astype(BF16)
-        act_copy = pltpu.make_async_copy(actb.at[s], out_act.at[s], local_sem.at[9 + s])
-        act_copy.start()
-        return act_copy
+                u3[s, j * 192 + kz * 64 : j * 192 + kz * 64 + 64, :] = rows.astype(BF16)
+        field = [u3[s, j * 192 : j * 192 + 192, :] for j in range(8)]
+        for j, back in enumerate(convolved(a3[...], field, 64)):
+            kb[s, 0, j] = back[0:16].astype(BF16)
+            bko[s, j] = back[16:48]
+            kb[s, 1, j] = back[48:64].astype(BF16)
+        pair = both_ways(4 + s, kb.at[s, 1], kh.at[s, 0], kb.at[s, 0], kh.at[s, 1])
+        for c in pair:
+            c.start()
+        out_act[s] = actf[...].reshape(32, 2, 8, 128).astype(BF16)
+        return pair
 
     def second_grad(s):
-        fields = [u2[s, (y + 1) * 288 + 48 : (y + 1) * 288 + 240, :] for y in range(8)]
+        fields = [u2[s, y * 192 : y * 192 + 192, :] for y in range(8)]
         deltas = [db[s, y : y + 3].reshape(192, 128) for y in range(8)]
         return dot_nt(jnp.concatenate(fields, axis=1), jnp.concatenate(deltas, axis=1))
 
-    def stage3(s):
-        parts = []
-        for j in range(4):
-            both = jnp.concatenate([u3[s, (2 * j + i) * 384 : (2 * j + i) * 384 + 384, :] for i in range(2)], axis=1)
-            part = dot(a3[...], both)
-            parts += [part[:, 0:128], part[:, 128:256]]
+    def stage3(s, pair):
+        arrive(pair, kh.at[s, 0], kh.at[s, 1])
         for j in range(8):
-            back = parts[j][32:64]
-            if j > 0:
-                back = back + parts[j - 1][0:32]
-            if j < 7:
-                back = back + parts[j + 1][64:96]
+            back = bko[s, j] + jnp.concatenate([kh[s, 0, j], kh[s, 1, j]], axis=0).astype(F32)
             for x in range(2):
                 bkf[pl.ds(x * 8 + j, 16, stride=16), :] = back[16 * x : 16 * x + 16]
             up = jnp.concatenate(doubled(back), axis=1)
             up = jnp.concatenate([up[0:16], up[0:16], up[16:32], up[16:32]], axis=0)
             for y in (2 * j, 2 * j + 1):
                 fd[s, y + 1] = (up * slope[s, y * 64 : y * 64 + 64, :]).astype(BF16)
-        bkb[s] = bkf[...].reshape(16, 2, 8, 128).astype(BF16)
-        copy = pltpu.make_async_copy(bkb.at[s], out_pg.at[s], local_sem.at[11 + s])
-        copy.start()
-        return copy
+        out_pg[s] = bkf[...].reshape(16, 2, 8, 128).astype(BF16)
 
     def first_grad(s):
         total = None
@@ -287,7 +298,7 @@
             ys = range(4 * k, 4 * k + 4)
             fields = [u1[s, (y + 1) * 80 : (y + 2) * 80, :] for y in ys]
             deltas = [fd[s, y : y + 3].reshape(192, 256) for y in ys]
-            part = dot_nt(jnp.concatenate(fields, axis=1), jnp.concatenate(deltas, axis=1))
+            part = dot_nt(jnp.concatenate(deltas, axis=1), jnp.concatenate(fields, axis=1))
             total = part if total is None else total + part
         return total
 
@@ -310,11 +321,9 @@
         lax.fori_loop(1, group, go, 0)
         return lambda: lax.fori_loop(1, group, end, 0)
 
-    pooled_pairs = [stage1(0), stage1(1)]
-    copies = [stage2(0, pooled_pairs[0]), stage3(0)]
-    acc1[:, 0:192] = first_grad(0)
+    near = [stage1(0), stage1(1)]
+    beside = [second_layer(s, near[s]) for s in range(2)]
     acc2[:, 0:192] = second_grad(0)
-    copies.append(stage2(1, pooled_pairs[1]))
     acc2[:, 0:192] += second_grad(1)
 
     lanes = lax.broadcasted_iota(jnp.int32, (144, 128), 1)
@@ -337,14 +346,21 @@
     r1[i1] = pack2[pl.ds(i1 * tp, tp)]
     scattered = exchange(0, g1, i1, peer1, lambda p: pack2.at[pl.ds(p * tp, tp)], r1.at[i1])
 
-    copies.append(stage3(1))
-    acc1[:, 0:192] += first_grad(1)
+    acc1[...] = jnp.zeros_like(acc1)
+    stage3(0, beside[0])
+    acc1[0:192, 0:80] += first_grad(0)
+    scattered()
+    r2[i2] = jnp.sum(r1[...], axis=0)
+    crossed = exchange(1, g2, i2, peer2, lambda p: r2.at[i2], r2.at[i2])
+    stage3(1, beside[1])
+    acc1[0:192, 0:80] += first_grad(1)
 
     rows = lax.broadcasted_iota(jnp.int32, (80, 128), 0)
     lanes = lax.broadcasted_iota(jnp.int32, (80, 128), 1)
     folded = []
+    turned = acc1[...].T[0:80]
     for half in range(2):
-        g = acc1[:, 128 * half : 128 * half + 128]
+        g = turned[:, 128 * half : 128 * half + 128]
         f1 = g
         for x in range(1, 4):
             f1 = f1 + pltpu.roll(pltpu.roll(g, 80 - 4 * x, 0), 128 - 16 * x, 1)
@@ -367,12 +383,11 @@
     packed = jnp.concatenate(packed, axis=0)
     p1[i1] = packed
     within = exchange(3, g1, i1, peer1, lambda p: p1.at[i1], p1.at[i1])
-    scattered()
-    r2[i2] = jnp.sum(r1[...], axis=0)
-    crossed = exchange(1, g2, i2, peer2, lambda p: r2.at[i2], r2.at[i2])
     within()
-    q1[i2] = jnp.sum(p1[...], axis=0)
-    over = exchange(4, g2, i2, peer2, lambda p: q1.at[i2], q1.at[i2])
+    pairs[core] = jnp.sum(p1[...], axis=0)
+    exchange(4, 2, core, peerc, lambda p: pairs.at[core], pairs.at[core])()
+    q1[iz] = pairs[0] + pairs[1]
+    over = exchange(5, g2 // 2, iz, peerz, lambda p: q1.at[iz], q1.at[iz])
     crossed()
     res[i1] = jnp.sum(r2[...], axis=0)
     gathered = exchange(2, g1, i1, peer1, lambda p: res.at[i1], res.at[i1])
@@ -380,28 +395,15 @@
     out_s1[...] = jnp.sum(q1[...], axis=0)
     gathered()
     out_s2[...] = res[...].reshape(128, 128)
-    for c in copies:
-        c.wait()
-
-
-def finish(
-    scales, act, pg, s1, s2, out_act, out_pg, out_g1, out_g2, actv, pgv, sums1, sums2, flat, g1v, g2v, sem
-):
-    loads = [
+
+
+def finish(scales, act, pg, sums1, sums2, out_act, out_pg, out_g1, out_g2, flat, g1v, g2v, sem):
+    stores = [
         pltpu.make_async_copy(src, dst, sem.at[k])
-        for k, (src, dst) in enumerate(((s1, sums1), (s2, sums2), (act, actv), (pg, pgv)))
+        for k, (src, dst) in enumerate(((act, out_act), (pg, out_pg), (g2v, out_g2), (g1v, out_g1)))
     ]
-    stores = [
-        pltpu.make_async_copy(src, dst, sem.at[4 + k])
-        for k, (src, dst) in enumerate(((actv, out_act), (pgv, out_pg), (g1v, out_g1), (g2v, out_g2)))
-    ]
-    for c in loads:
+    for c in stores[0:2]:
         c.start()
-    for k in (2, 3):
-        loads[k].wait()
-        stores[k - 2].start()
-    for c in loads[0:2]:
-        c.wait()
     total = sums2[...] * scales[1]
     rest = pltpu.roll(total[0:48], 32, 1)
     for ky in range(3):
@@ -409,6 +411,7 @@
         whole = jnp.concatenate([part, rest[ky * 16 : ky * 16 + 16]], axis=0)[:, 0:32]
         for kx in range(3):
             g2v[kx, ky] = whole[kx * 48 : kx * 48 + 48].reshape(3, 16, 32)
+    stores[2].start()
     total = sums1[...] * scales[0]
     for k in range(15):
         part = total[8 * (k % 2) : 8 * (k % 2) + 8]
@@ -418,8 +421,7 @@
             for kz in range(3):
                 row = (2 - ky) * 40 + kz * 12 + kx * 4
                 g1v[kx, ky, kz] = flat[row : row + 4, 0:16]
-    for c in stores[2:]:
-        c.start()
+    stores[3].start()
     for c in stores:
         c.wait()
 
@@ -433,58 +435,60 @@
         w1 = jnp.transpose(first_kernel, (2, 3, 4, 1, 0))
         w2 = jnp.transpose(second_kernel, (2, 3, 4, 1, 0))
         hbm = pl.BlockSpec(memory_space=pltpu.HBM)
+        vmem = pl.BlockSpec(memory_space=pltpu.VMEM)
         g1 = sizes[0][0] * sizes[0][2]
         g2 = sizes[0][1] * sizes[1]
-        vmem_limit = 60 * 1024 * 1024
+        vmem_limit = 63 * 1024 * 1024
         act, pooled_grad, sums1, sums2 = pl.pallas_call(
             functools.partial(kernel, sizes),
             out_shape=(
-                jax.ShapeDtypeStruct((2, 32, 2, 8, 128), BF16),
-                jax.ShapeDtypeStruct((2, 16, 2, 8, 128), BF16),
-                jax.ShapeDtypeStruct((16, 128), F32),
-                jax.ShapeDtypeStruct((128, 128), F32),
+                pltpu.VMEM((2, 32, 2, 8, 128), BF16),
+                pltpu.VMEM((2, 16, 2, 8, 128), BF16),
+                pltpu.VMEM((16, 128), F32),
+                pltpu.VMEM((128, 128), F32),
             ),
             in_specs=[hbm] * 4,
-            out_specs=(hbm, hbm, pl.BlockSpec(memory_space=pltpu.VMEM), pl.BlockSpec(memory_space=pltpu.VMEM)),
+            out_specs=(vmem,) * 4,
             scratch_shapes=[
                 pltpu.VMEM((2, 6, 4, 16, 256), BF16),
                 pltpu.VMEM((2, 384, 128), F32),
                 pltpu.VMEM((2, 1456, 256), BF16),
                 pltpu.VMEM((2, 1024, 256), F32),
-                pltpu.VMEM((2, 8, 2, 16, 128), BF16),
-                pltpu.VMEM((2, 2, 8, 2, 16, 128), BF16),
-                pltpu.VMEM((2, 2912, 128), BF16),
+                pltpu.VMEM((2, 2, 8, 16, 128), BF16),
+                pltpu.VMEM((2, 2, 8, 16, 128), BF16),
+                pltpu.VMEM((2, 1536, 128), BF16),
                 pltpu.VMEM((2, 32, 2, 8, 128), BF16),
-                pltpu.VMEM((2, 2, 32, 8, 128), BF16),
-                pltpu.VMEM((4, 256, 128), F32),
+                pltpu.VMEM((2, 256, 128), F32),
                 pltpu.VMEM((512, 128), F32),
-                pltpu.VMEM((2, 32, 2, 8, 128), BF16),
                 pltpu.VMEM((2, 10, 64, 128), BF16),
                 pltpu.VMEM((2, 18, 64, 256), BF16),
-                pltpu.VMEM((2, 3072, 128), BF16),
+                pltpu.VMEM((2, 1536, 128), BF16),
+                pltpu.VMEM((2, 8, 32, 128), F32),
+                pltpu.VMEM((2, 2, 8, 16, 128), BF16),
+                pltpu.VMEM((2, 2, 8, 16, 128), BF16),
                 pltpu.VMEM((256, 128), F32),
-                pltpu.VMEM((2, 16, 2, 8, 128), BF16),
                 pltpu.VMEM((3, 3, 3, 4, 16), BF16),
                 pltpu.VMEM((3, 3, 3, 16, 32), BF16),
                 pltpu.VMEM((256, 128), F32),
-                pltpu.VMEM((896, 128), F32),
+                pltpu.VMEM((3, 256, 128), F32),
                 pltpu.VMEM((432, 128), F32),
                 pltpu.VMEM((64, 256), BF16),
-                pltpu.VMEM((128, 896), BF16),
-                pltpu.VMEM((96, 384), BF16),
-                pltpu.VMEM((80, 256), F32),
+                pltpu.VMEM((192, 192), BF16),
+                pltpu.VMEM((192, 192), BF16),
+                pltpu.VMEM((256, 128), F32),
                 pltpu.VMEM((192, 256), F32),
                 pltpu.VMEM((16, 8, 128), F32),
                 pltpu.VMEM((g1, 16, 128), F32),
-                pltpu.VMEM((g2, 16, 128), F32),
+                pltpu.VMEM((2, 16, 128), F32),
+                pltpu.VMEM((g2 // 2, 16, 128), F32),
                 pltpu.VMEM((g1, 16 // g1, 8, 128), F32),
                 pltpu.VMEM((g2, 16 // g1, 8, 128), F32),
                 pltpu.VMEM((g1, 16 // g1, 8, 128), F32),
-                pltpu.SemaphoreType.DMA((15,)),
+                pltpu.SemaphoreType.DMA((11,)),
                 pltpu.SemaphoreType.DMA((6, 2)),
                 pltpu.SemaphoreType.DMA((6, 2)),
-                pltpu.SemaphoreType.DMA((5, max(g1, g2))),
-                pltpu.SemaphoreType.DMA((5, max(g1, g2))),
+                pltpu.SemaphoreType.DMA((6, max(g1, g2))),
+                pltpu.SemaphoreType.DMA((6, max(g1, g2))),
             ],
             compiler_params=pltpu.CompilerParams(
                 collective_id=0, has_side_effects=True, vmem_limit_bytes=vmem_limit
@@ -498,19 +502,15 @@
                 jax.ShapeDtypeStruct((3, 3, 3, 4, 16), F32),
                 jax.ShapeDtypeStruct((3, 3, 3, 16, 32), F32),
             ),
-            in_specs=[hbm] * 4,
+            in_specs=[vmem] * 4,
             out_specs=(hbm,) * 4,
             scratch_shapes=[
-                pltpu.VMEM((2, 32, 2, 8, 128), BF16),
-                pltpu.VMEM((2, 16, 2, 8, 128), BF16),
-                pltpu.VMEM((16, 128), F32),
-                pltpu.VMEM((128, 128), F32),
                 pltpu.VMEM((128, 128), F32),
                 pltpu.VMEM((3, 3, 3, 4, 16), F32),
                 pltpu.VMEM((3, 3, 3, 16, 32), F32),
-                pltpu.SemaphoreType.DMA((8,)),
+                pltpu.SemaphoreType.DMA((4,)),
             ],
-            compiler_params=pltpu.CompilerParams(vmem_limit_bytes=vmem_limit),
+            compiler_params=pltpu.CompilerParams(vmem_limit_bytes=16 * 1024 * 1024),
         )(act, pooled_grad, sums1, sums2)
         return (
             act,

time: 50.8 us -> 48.3 us (0.951)
  Pallas kernels: 50 us -> 47.5 us
    pallas_call x1, Pallas kernels: 48.1 us -> 46.6 us  [body(): pl.pallas_call(functools.partial(kernel, sizes), out_shape=(pltpu.VMEM((2...]
    pallas_call x1, Pallas kernels: 1.93 us -> 0.87 us  [body(): pl.pallas_call(functools.partial(finish, scales), out_shape=(jax.ShapeDty...]
where the time goes in v3:
time: 48.3 us; the launch traced here: 48.2 us
  Pallas kernels  47.5 us (98%)
  between operations  0.64 us (1%)
    pallas_call x1, Pallas kernels, body(): pl.pallas_call(functools.partial(kernel, sizes), out_shape=(pltpu.VMEM((2...  46.6 us

profile of v3, /device:TPU:1, one launch (start us, length us, event | category | flops | bytes accessed | tf_op | source)
XLA Modules:
  0.0 48.2 jit_solution(14120350625307688335)
XLA Ops:
  0.6 46.6 %shard_map.75 = (bf16[2,32,2,8,128]{4,3,2,1,0:T(8,128)(2,1)S(1)}, bf16[2,16,2,8,128]{4,3,2,1,0:T(8,128)(2,1)S(1)}, f32[16,128]{1,0:T(8,128)S(1)}, f32[128,128]{1,0:T(8,128)S(1)}) custom-call(bf16[2,4,4,16,256]{4,3,2,1,0:T(8,128)(2,1)} %vol.1, bf16[3,3,3,4,16]{4,3,2,1,0:T(4,128)(2,1)} %bitcast.5, bf16[3,3,3,16,32]{4,3,2,1,0:T(8,128)(2,1)} %bitcast.4, ...), custom_call_target="tpu_custom_call" | custom-call | tf_op jit(solution)/shard_map/pallas_call | solution.py:442
  47.3 0.9 %shard_map.76 = (bf16[2,32,2,8,128]{4,3,2,1,0:T(8,128)(2,1)}, bf16[2,16,2,8,128]{4,3,2,1,0:T(8,128)(2,1)}, f32[3,3,3,4,16]{4,3,2,1,0:T(4,128)}, f32[3,3,3,16,32]{4,3,2,1,0:T(8,128)}) custom-call(bf16[2,32,2,8,128]{4,3,2,1,0:T(8,128)(2,1)S(1)} %get-tuple-element.12.act, bf16[2,16,2,8,128]{4,3,2,1,0:T(8,128)(2,1)S(1)} %get-tuple-element.13.pg, ...), custom_call_target="tpu_custom_call" | custom-call | tf_op jit(solution)/shard_map/pallas_call | solution.py:497

commit v4 on v3

--- a/solution.py
+++ b/solution.py
@@ -18,6 +18,18 @@
     if side**3 == count:
         return side, side, side
     return 2, 1, count // 2
+
+
+def hops(step, count):
+    return min(step, count - step)
+
+
+def offsets(nx, ny, nz, cores):
+    steps = [
+        (dx, dy, dz, dc) for dx in range(nx) for dy in range(ny) for dz in range(nz) for dc in range(cores)
+    ]
+    far = lambda d: hops(d[0], nx) + hops(d[1], ny) + hops(d[2], nz) + 0.1 * d[3]
+    return sorted(steps[1:], key=far, reverse=True)
 
 
 def dot(a, b):
@@ -60,67 +72,58 @@
 
 def kernel(
     sizes, vol, w1_hbm, w2_hbm, cot, out_act, out_pg, out_s1, out_s2,
-    vbuf, vf, u1, slope, pb, ph, u2, cotb, cotf, actf, db, fd, u3, bko, kb, kh, bkf,
-    w1, w2, a1s, a2s, w2f, a1, a2, a3, acc1, acc2, pack2, p1, pairs, q1, r1, r2, res,
+    vbuf, vf, u1, slope, pb, ph, u2, cotb, ch, cotf, actf, db, fd, u3, bkf,
+    w1, w2, a1s, a2s, w2f, a1, a2, a2h, a3, acc1, acc2, pack2, p1, q1, r1, r2, res,
     local_sem, halo_send, halo_recv, sum_send, sum_recv,
 ):
     (nx, nzh, ny), nb = sizes
     n_space = nx * nzh * ny
-    g1, g2 = nx * ny, nzh * nb
+    g1 = nx * ny
     tp = 16 // g1
     sp, bt = lax.axis_index("space"), lax.axis_index("batch")
     xi = lax.div(sp, nzh * ny)
     zi = lax.rem(lax.div(sp, ny), nzh)
     yi = lax.rem(sp, ny)
     i1 = xi * ny + yi
-    i2 = zi * nb + bt
     core = lax.rem(bt, 2)
-    zlow = lax.div(bt, 2)
-    iz = zi * (nb // 2) + zlow
+    nzl = nb // 2
+    nz = nzh * nzl
+    iz = zi * nzl + lax.div(bt, 2)
     right = lax.rem(sp + 1, n_space)
     left = lax.rem(sp + n_space - 1, n_space)
 
-    def peer1(p):
-        return (lax.div(p, ny) * (nzh * ny) + zi * ny + lax.rem(p, ny), bt)
-
-    def peer2(p):
-        return (xi * (nzh * ny) + lax.div(p, nb) * ny + yi, lax.rem(p, nb))
-
-    def peerz(p):
-        low = nb // 2
-        return (xi * (nzh * ny) + lax.div(p, low) * ny + yi, lax.rem(p, low) * 2 + core)
-
-    def peerc(p):
-        return (sp, zlow * 2 + p)
+    def at(step):
+        dx, dy, dz, dc = step
+        x, y, z, c = lax.rem(xi + dx, nx), lax.rem(yi + dy, ny), lax.rem(iz + dz, nz), lax.rem(core + dc, 2)
+        place = (x * (nzh * ny) + lax.div(z, nzl) * ny + y, lax.rem(z, nzl) * 2 + c)
+        return place, x * ny + y, c
+
+    slab_group = offsets(nx, ny, 1, 1)
+    column = offsets(1, 1, nz, 2)
 
     barrier = pltpu.get_barrier_semaphore()
     for side in (left, right):
         pl.semaphore_signal(barrier, inc=1, device_id=(side, bt), device_id_type=MESH)
 
-    def greet1(d, c):
-        pl.semaphore_signal(barrier, inc=1, device_id=peer1(lax.rem(i1 + d, g1)), device_id_type=MESH)
-        return c
-
-    def greet2(d, c):
-        pl.semaphore_signal(barrier, inc=1, device_id=peer2(lax.rem(i2 + d, g2)), device_id_type=MESH)
-        return c
-
-    lax.fori_loop(1, g1, greet1, 0)
-    lax.fori_loop(1, g2, greet2, 0)
+    others = slab_group + column
+    for step in others:
+        pl.semaphore_signal(barrier, inc=1, device_id=at(step)[0], device_id_type=MESH)
 
     own = []
     for s in range(2):
         for x in range(4):
             own.append(pltpu.make_async_copy(vol.at[s, :, x], vbuf.at[s, x + 1], local_sem.at[s * 4 + x]))
-    own.append(pltpu.make_async_copy(cot, cotb, local_sem.at[8]))
-    own.append(pltpu.make_async_copy(w1_hbm, w1, local_sem.at[9]))
-    own.append(pltpu.make_async_copy(w2_hbm, w2, local_sem.at[10]))
+    for s in range(2):
+        for x in range(2):
+            own.append(pltpu.make_async_copy(cot.at[s, :, x], cotb.at[s, x], local_sem.at[8 + s * 2 + x]))
+    own.append(pltpu.make_async_copy(w1_hbm, w1, local_sem.at[12]))
+    own.append(pltpu.make_async_copy(w2_hbm, w2, local_sem.at[13]))
     for c in own:
         c.start()
     for c in own[0:8]:
         c.wait()
 
-    pl.semaphore_wait(barrier, 2 + g1 - 1 + g2 - 1)
+    pl.semaphore_wait(barrier, 2 + len(others))
 
     def both_ways(k, to_right, land_right, to_left, land_left):
         one = pltpu.make_async_remote_copy(
@@ -139,6 +142,9 @@
             c.start()
     for c in own[8:]:
         c.wait()
+    cot_pairs = [both_ways(6 + s, cotb.at[s, 1], ch.at[s, 0], cotb.at[s, 0], ch.at[s, 1]) for s in range(2)]
+    for c in cot_pairs[0]:
+        c.start()
 
     def arrive(pair, low, high):
         for c in pair:
@@ -173,16 +179,15 @@
         base = a2s[ky]
         both = (base + pltpu.roll(pltpu.roll(base, 48, 0), 32, 1)).T[0:64, 0:192].astype(BF16)
         a2[64 * ky : 64 * ky + 64, :] = both
+        for x in range(2):
+            a2h[x, 32 * ky : 32 * ky + 32, :] = both[32 * x : 32 * x + 32]
     for ky in range(3):
-        pieces = []
         for kz in range(3):
             rows = [((kx * 3 + 2 - ky) * 3 + 2 - kz) * 16 for kx in range(3)]
-            zero = jnp.zeros((16, 128), F32)
-            kept = [w2f[r : r + 16, :] for r in rows] + [zero]
-            both = jnp.concatenate(kept, axis=0) + pltpu.roll(jnp.concatenate([zero] + kept[0:3], axis=0), 32, 1)
-            pieces.append(both)
-        a3[64 * ky : 64 * ky + 64, 0:128] = (pieces[0] + pltpu.roll(pieces[1], 64, 1)).astype(BF16)
-        a3[64 * ky : 64 * ky + 64, 128:192] = pieces[2][:, 0:64].astype(BF16)
+            blocks = [w2f[r : r + 16, :] for r in rows]
+            first = blocks[2] + pltpu.roll(blocks[1], 32, 1) + pltpu.roll(blocks[0], 64, 1)
+            both = jnp.concatenate([first, pltpu.roll(first, 32, 1)], axis=0)
+            a3[32 * ky : 32 * ky + 32, kz * 128 : kz * 128 + 128] = both.astype(BF16)
 
     for s in range(2):
         u1[s, 0:80, :] = jnp.zeros((80, 256), BF16)
@@ -219,17 +224,28 @@
             for x in range(2):
                 part = slice(16 * x, 16 * x + 16)
                 rows = jnp.concatenate([before[part], mid[part], after[part]], axis=0)
-                at = j * 192 + (x + 1) * 48
+                at = j * 288 + (x + 2) * 48
                 u2[s, at : at + 48, :] = rows.astype(BF16)
-        near = both_ways(2 + s, pb.at[s, 1], ph.at[s, 0], pb.at[s, 0], ph.at[s, 1])
+        near = both_ways(2 + s, pb.at[s, 1], ph.at[s, 0, 1], pb.at[s, 0], ph.at[s, 1, 0])
+        far = both_ways(4 + s, pb.at[s, 0], ph.at[s, 0, 0], pb.at[s, 1], ph.at[s, 1, 1])
         for c in near:
             c.start()
-        return near
-
-    def convolved(matrix, field, count):
+        return near, far
+
+    def fill(s, planes):
+        for j in range(8):
+            mid = jnp.concatenate([ph[s, side, x, j] for side, x, at in planes], axis=0).astype(F32)
+            before, after = shifts(mid)
+            for k, (side, x, at) in enumerate(planes):
+                part = slice(16 * k, 16 * k + 16)
+                rows = jnp.concatenate([before[part], mid[part], after[part]], axis=0)
+                u2[s, j * 288 + at * 48 : j * 288 + at * 48 + 48, :] = rows.astype(BF16)
+
+    def convolved(s, matrix, first, count):
         parts = []
         for j in range(4):
-            part = dot(matrix, jnp.concatenate([field[2 * j], field[2 * j + 1]], axis=1))
+            both = [u2[s, (2 * j + i) * 288 + first : (2 * j + i) * 288 + first + 192, :] for i in range(2)]
+            part = dot(matrix, jnp.concatenate(both, axis=1))
             parts += [part[:, 0:128], part[:, 128:256]]
         out = []
         for j in range(8):
@@ -241,49 +257,61 @@
             out.append(pre)
         return out
 
-    def second_layer(s, near):
+    def spread_delta(s, j, delta, places):
+        mid = delta.astype(F32)
+        before, after = shifts(mid)
+        for kz, rows in enumerate((before, mid, after)):
+            rows = rows.astype(BF16)
+            for first, count, at in places:
+                low = j * 384 + kz * 128 + at
+                u3[s, low : low + count, :] = rows[first : first + count]
+
+    def second_own(s, near):
         for x in range(2):
-            cotf[x] = cotb[s, :, x].reshape(256, 128).astype(F32)
-        arrive(near, ph.at[s, 0], ph.at[s, 1])
-        for j in range(8):
-            mid = jnp.concatenate([ph[s, 0, j], ph[s, 1, j]], axis=0).astype(F32)
-            before, after = shifts(mid)
-            for side in range(2):
-                part = slice(16 * side, 16 * side + 16)
-                rows = jnp.concatenate([before[part], mid[part], after[part]], axis=0)
-                u2[s, j * 192 + side * 144 : j * 192 + side * 144 + 48, :] = rows.astype(BF16)
-        field = [u2[s, j * 192 : j * 192 + 192, :] for j in range(8)]
-        for j, pre in enumerate(convolved(a2[...], field, 64)):
+            cotf[x + 1] = cotb[s, x].reshape(256, 128).astype(F32)
+        arrive(near, ph.at[s, 0, 1], ph.at[s, 1, 0])
+        fill(s, ((0, 1, 1), (1, 0, 4)))
+        for j, pre in enumerate(convolved(s, a2[...], 48, 64)):
             act, sl = act_and_slope(pre)
             for x in range(2):
                 actf[pl.ds(x * 8 + j, 32, stride=16), :] = act[32 * x : 32 * x + 32]
-            got = [cotf[x, pl.ds(j, 32, stride=8), :] for x in range(2)]
+            got = [cotf[1 + x, pl.ds(j, 32, stride=8), :] for x in range(2)]
             delta = (jnp.concatenate(got, axis=0) * sl).astype(BF16)
             db[s, j + 1] = delta
-            mid = delta.astype(F32)
-            before, after = shifts(mid)
-            for kz, rows in enumerate((before, mid, after)):
-                u3[s, j * 192 + kz * 64 : j * 192 + kz * 64 + 64, :] = rows.astype(BF16)
-        field = [u3[s, j * 192 : j * 192 + 192, :] for j in range(8)]
-        for j, back in enumerate(convolved(a3[...], field, 64)):
-            kb[s, 0, j] = back[0:16].astype(BF16)
-            bko[s, j] = back[16:48]
-            kb[s, 1, j] = back[48:64].astype(BF16)
-        pair = both_ways(4 + s, kb.at[s, 1], kh.at[s, 0], kb.at[s, 0], kh.at[s, 1])
-        for c in pair:
-            c.start()
+            spread_delta(s, j, delta, ((0, 64, 32),))
         out_act[s] = actf[...].reshape(32, 2, 8, 128).astype(BF16)
-        return pair
+
+    def second_beside(s, far):
+        arrive(cot_pairs[s], ch.at[s, 0], ch.at[s, 1])
+        for side in range(2):
+            cotf[3 * side] = ch[s, side].reshape(256, 128).astype(F32)
+        arrive(far, ph.at[s, 0, 0], ph.at[s, 1, 1])
+        fill(s, ((0, 0, 0), (1, 1, 5)))
+        low = convolved(s, a2h[0], 0, 32)
+        high = convolved(s, a2h[1], 96, 32)
+        for j in range(8):
+            sl = act_and_slope(jnp.concatenate([low[j], high[j]], axis=0))[1]
+            got = [cotf[3 * side, pl.ds(j, 32, stride=8), :] for side in range(2)]
+            delta = (jnp.concatenate(got, axis=0) * sl).astype(BF16)
+            spread_delta(s, j, delta, ((0, 32, 0), (32, 32, 96)))
 
     def second_grad(s):
-        fields = [u2[s, y * 192 : y * 192 + 192, :] for y in range(8)]
+        fields = [u2[s, y * 288 + 48 : y * 288 + 240, :] for y in range(8)]
         deltas = [db[s, y : y + 3].reshape(192, 128) for y in range(8)]
         return dot_nt(jnp.concatenate(fields, axis=1), jnp.concatenate(deltas, axis=1))
 
-    def stage3(s, pair):
-        arrive(pair, kh.at[s, 0], kh.at[s, 1])
+    def stage3(s):
+        parts = []
+        for j in range(4):
+            both = jnp.concatenate([u3[s, (2 * j + i) * 384 : (2 * j + i) * 384 + 384, :] for i in range(2)], axis=1)
+            part = dot(a3[...], both)
+            parts += [part[:, 0:128], part[:, 128:256]]
         for j in range(8):
-            back = bko[s, j] + jnp.concatenate([kh[s, 0, j], kh[s, 1, j]], axis=0).astype(F32)
+            back = parts[j][32:64]
+            if j > 0:
+                back = back + parts[j - 1][0:32]
+            if j < 7:
+                back = back + parts[j + 1][64:96]
             for x in range(2):
                 bkf[pl.ds(x * 8 + j, 16, stride=16), :] = back[16 * x : 16 * x + 16]
             up = jnp.concatenate(doubled(back), axis=1)
@@ -302,28 +330,29 @@
             total = part if total is None else total + part
         return total
 
-    def exchange(phase, group, index, peer, src, dst):
-        def make(d):
-            other = lax.rem(index + d, group)
-            return pltpu.make_async_remote_copy(
-                src_ref=src(other), dst_ref=dst, send_sem=sum_send.at[phase, d], recv_sem=sum_recv.at[phase, d],
-                device_id=peer(other), device_id_type=MESH,
+    def exchange(phase, group, src, dst):
+        sent = []
+        for k, step in enumerate(group):
+            place, slab, c = at(step)
+            copy = pltpu.make_async_remote_copy(
+                src_ref=src(slab, c), dst_ref=dst, send_sem=sum_send.at[phase, k], recv_sem=sum_recv.at[phase, k],
+                device_id=place, device_id_type=MESH,
             )
-
-        def go(d, c):
-            make(d).start()
-            return c
-
-        def end(d, c):
-            make(d).wait()
-            return c
-
-        lax.fori_loop(1, group, go, 0)
-        return lambda: lax.fori_loop(1, group, end, 0)
-
-    near = [stage1(0), stage1(1)]
-    beside = [second_layer(s, near[s]) for s in range(2)]
+            copy.start()
+            sent.append(copy)
+
+        def finished():
+            for copy in sent:
+                copy.wait()
+
+        return finished
+
+    halves = [stage1(0), stage1(1)]
+    for c in (*halves[0][1], *cot_pairs[1], *halves[1][1]):
+        c.start()
+    second_own(0, halves[0][0])
     acc2[:, 0:192] = second_grad(0)
+    second_own(1, halves[1][0])
     acc2[:, 0:192] += second_grad(1)
 
     lanes = lax.broadcasted_iota(jnp.int32, (144, 128), 1)
@@ -344,16 +373,13 @@
     pack2[...] = (f2[0:128] + rest).reshape(16, 8, 128)
 
     r1[i1] = pack2[pl.ds(i1 * tp, tp)]
-    scattered = exchange(0, g1, i1, peer1, lambda p: pack2.at[pl.ds(p * tp, tp)], r1.at[i1])
+    scattered = exchange(0, slab_group, lambda slab, c: pack2.at[pl.ds(slab * tp, tp)], r1.at[i1])
 
     acc1[...] = jnp.zeros_like(acc1)
-    stage3(0, beside[0])
-    acc1[0:192, 0:80] += first_grad(0)
-    scattered()
-    r2[i2] = jnp.sum(r1[...], axis=0)
-    crossed = exchange(1, g2, i2, peer2, lambda p: r2.at[i2], r2.at[i2])
-    stage3(1, beside[1])
-    acc1[0:192, 0:80] += first_grad(1)
+    for s in range(2):
+        second_beside(s, halves[s][1])
+        stage3(s)
+        acc1[0:192, 0:80] += first_grad(s)
 
     rows = lax.broadcasted_iota(jnp.int32, (80, 128), 0)
     lanes = lax.broadcasted_iota(jnp.int32, (80, 128), 1)
@@ -382,15 +408,16 @@
             packed[k % 2] = part if packed[k % 2] is None else packed[k % 2] + part
     packed = jnp.concatenate(packed, axis=0)
     p1[i1] = packed
-    within = exchange(3, g1, i1, peer1, lambda p: p1.at[i1], p1.at[i1])
+    within = exchange(3, slab_group, lambda slab, c: p1.at[i1], p1.at[i1])
+    scattered()
+    r2[iz * 2 + core] = jnp.sum(r1[...], axis=0)
+    crossed = exchange(1, column, lambda slab, c: r2.at[iz * 2 + core], r2.at[iz * 2 + core])
     within()
-    pairs[core] = jnp.sum(p1[...], axis=0)
-    exchange(4, 2, core, peerc, lambda p: pairs.at[core], pairs.at[core])()
-    q1[iz] = pairs[0] + pairs[1]
-    over = exchange(5, g2 // 2, iz, peerz, lambda p: q1.at[iz], q1.at[iz])
+    q1[iz * 2 + core] = jnp.sum(p1[...], axis=0)
+    over = exchange(4, column, lambda slab, c: q1.at[iz * 2 + core], q1.at[iz * 2 + core])
     crossed()
     res[i1] = jnp.sum(r2[...], axis=0)
-    gathered = exchange(2, g1, i1, peer1, lambda p: res.at[i1], res.at[i1])
+    gathered = exchange(2, slab_group, lambda slab, c: res.at[i1], res.at[i1])
     over()
     out_s1[...] = jnp.sum(q1[...], axis=0)
     gathered()
@@ -455,17 +482,15 @@
                 pltpu.VMEM((2, 1456, 256), BF16),
                 pltpu.VMEM((2, 1024, 256), F32),
                 pltpu.VMEM((2, 2, 8, 16, 128), BF16),
-                pltpu.VMEM((2, 2, 8, 16, 128), BF16),
-                pltpu.VMEM((2, 1536, 128), BF16),
-                pltpu.VMEM((2, 32, 2, 8, 128), BF16),
-                pltpu.VMEM((2, 256, 128), F32),
+                pltpu.VMEM((2, 2, 2, 8, 16, 128), BF16),
+                pltpu.VMEM((2, 2304, 128), BF16),
+                pltpu.VMEM((2, 2, 32, 8, 128), BF16),
+                pltpu.VMEM((2, 2, 32, 8, 128), BF16),
+                pltpu.VMEM((4, 256, 128), F32),
                 pltpu.VMEM((512, 128), F32),
                 pltpu.VMEM((2, 10, 64, 128), BF16),
                 pltpu.VMEM((2, 18, 64, 256), BF16),
-                pltpu.VMEM((2, 1536, 128), BF16),
-                pltpu.VMEM((2, 8, 32, 128), F32),
-                pltpu.VMEM((2, 2, 8, 16, 128), BF16),
-                pltpu.VMEM((2, 2, 8, 16, 128), BF16),
+                pltpu.VMEM((2, 3072, 128), BF16),
                 pltpu.VMEM((256, 128), F32),
                 pltpu.VMEM((3, 3, 3, 4, 16), BF16),
                 pltpu.VMEM((3, 3, 3, 16, 32), BF16),
@@ -474,21 +499,21 @@
                 pltpu.VMEM((432, 128), F32),
                 pltpu.VMEM((64, 256), BF16),
                 pltpu.VMEM((192, 192), BF16),
-                pltpu.VMEM((192, 192), BF16),
+                pltpu.VMEM((2, 96, 192), BF16),
+                pltpu.VMEM((96, 384), BF16),
                 pltpu.VMEM((256, 128), F32),
                 pltpu.VMEM((192, 256), F32),
                 pltpu.VMEM((16, 8, 128), F32),
                 pltpu.VMEM((g1, 16, 128), F32),
-                pltpu.VMEM((2, 16, 128), F32),
-                pltpu.VMEM((g2 // 2, 16, 128), F32),
+                pltpu.VMEM((g2, 16, 128), F32),
                 pltpu.VMEM((g1, 16 // g1, 8, 128), F32),
                 pltpu.VMEM((g2, 16 // g1, 8, 128), F32),
                 pltpu.VMEM((g1, 16 // g1, 8, 128), F32),
-                pltpu.SemaphoreType.DMA((11,)),
-                pltpu.SemaphoreType.DMA((6, 2)),
-                pltpu.SemaphoreType.DMA((6, 2)),
-                pltpu.SemaphoreType.DMA((6, max(g1, g2))),
-                pltpu.SemaphoreType.DMA((6, max(g1, g2))),
+                pltpu.SemaphoreType.DMA((14,)),
+                pltpu.SemaphoreType.DMA((8, 2)),
+                pltpu.SemaphoreType.DMA((8, 2)),
+                pltpu.SemaphoreType.DMA((5, max(g1, g2))),
+                pltpu.SemaphoreType.DMA((5, max(g1, g2))),
             ],
             compiler_params=pltpu.CompilerParams(
                 collective_id=0, has_side_effects=True, vmem_limit_bytes=vmem_limit

time: 48.3 us -> 47.2 us (0.977)
  Pallas kernels: 47.5 us -> 46.5 us
    pallas_call x1, Pallas kernels: 46.6 us -> 45.6 us  [body(): pl.pallas_call(functools.partial(kernel, sizes), out_shape=(pltpu.VMEM((2...]
where the time goes in v4:
time: 47.2 us; the launch traced here: 47.1 us
  Pallas kernels  46.5 us (99%)
  between operations  0.64 us (1%)
    pallas_call x1, Pallas kernels, body(): pl.pallas_call(functools.partial(kernel, sizes), out_shape=(pltpu.VMEM((2...  45.6 us

profile of v4, /device:TPU:1, one launch (start us, length us, event | category | flops | bytes accessed | tf_op | source)
XLA Modules:
  0.0 47.1 jit_solution(1159609679907651781)
XLA Ops:
  0.6 45.6 %shard_map.75 = (bf16[2,32,2,8,128]{4,3,2,1,0:T(8,128)(2,1)S(1)}, bf16[2,16,2,8,128]{4,3,2,1,0:T(8,128)(2,1)S(1)}, f32[16,128]{1,0:T(8,128)S(1)}, f32[128,128]{1,0:T(8,128)S(1)}) custom-call(bf16[2,4,4,16,256]{4,3,2,1,0:T(8,128)(2,1)} %vol.1, bf16[3,3,3,4,16]{4,3,2,1,0:T(4,128)(2,1)} %bitcast.5, bf16[3,3,3,16,32]{4,3,2,1,0:T(8,128)(2,1)} %bitcast.4, ...), custom_call_target="tpu_custom_call" | custom-call | tf_op jit(solution)/shard_map/pallas_call | solution.py:469
  46.3 0.9 %shard_map.76 = (bf16[2,32,2,8,128]{4,3,2,1,0:T(8,128)(2,1)}, bf16[2,16,2,8,128]{4,3,2,1,0:T(8,128)(2,1)}, f32[3,3,3,4,16]{4,3,2,1,0:T(4,128)}, f32[3,3,3,16,32]{4,3,2,1,0:T(8,128)}) custom-call(bf16[2,32,2,8,128]{4,3,2,1,0:T(8,128)(2,1)S(1)} %get-tuple-element.12.act, bf16[2,16,2,8,128]{4,3,2,1,0:T(8,128)(2,1)S(1)} %get-tuple-element.13.pg, ...), custom_call_target="tpu_custom_call" | custom-call | tf_op jit(solution)/shard_map/pallas_call | solution.py:522

commit v5 on v4

--- a/solution.py
+++ b/solution.py
@@ -106,7 +106,8 @@
         pl.semaphore_signal(barrier, inc=1, device_id=(side, bt), device_id_type=MESH)
 
     others = slab_group + column
-    for step in others:
+    near = lambda d: hops(d[0], nx) + hops(d[1], ny) + hops(d[2], nz) + 0.1 * d[3]
+    for step in sorted(others, key=near, reverse=True):
         pl.semaphore_signal(barrier, inc=1, device_id=at(step)[0], device_id_type=MESH)
 
     own = []
@@ -143,12 +144,10 @@
     for c in own[8:]:
         c.wait()
     cot_pairs = [both_ways(6 + s, cotb.at[s, 1], ch.at[s, 0], cotb.at[s, 0], ch.at[s, 1]) for s in range(2)]
-    for c in cot_pairs[0]:
-        c.start()
 
     def arrive(pair, low, high):
         for c in pair:
-            c.wait()
+            c.wait_recv()
 
         @pl.when(sp == 0)
         def _():
@@ -196,6 +195,15 @@
             db[s, y] = jnp.zeros((64, 128), BF16)
         for y in (0, 17):
             fd[s, y] = jnp.zeros((64, 256), BF16)
+
+    def sent_off(*pairs):
+        for pair in pairs:
+            for c in pair:
+                c.wait_send()
+
+    sent_off(*halos)
+    for c in (*cot_pairs[0], *cot_pairs[1]):
+        c.start()
 
     def stage1(s):
         arrive(halos[s], vbuf.at[s, 0], vbuf.at[s, 5])
@@ -274,12 +282,14 @@
         for j, pre in enumerate(convolved(s, a2[...], 48, 64)):
             act, sl = act_and_slope(pre)
             for x in range(2):
-                actf[pl.ds(x * 8 + j, 32, stride=16), :] = act[32 * x : 32 * x + 32]
+                actf[s, pl.ds(x * 8 + j, 32, stride=16), :] = act[32 * x : 32 * x + 32]
             got = [cotf[1 + x, pl.ds(j, 32, stride=8), :] for x in range(2)]
-            delta = (jnp.concatenate(got, axis=0) * sl).astype(BF16)
-            db[s, j + 1] = delta
-            spread_delta(s, j, delta, ((0, 64, 32),))
-        out_act[s] = actf[...].reshape(32, 2, 8, 128).astype(BF16)
+            db[s, j + 1] = (jnp.concatenate(got, axis=0) * sl).astype(BF16)
+
+    def after_own(s):
+        out_act[s] = actf[s].reshape(32, 2, 8, 128).astype(BF16)
+        for j in range(8):
+            spread_delta(s, j, db[s, j + 1], ((0, 64, 32),))
 
     def second_beside(s, far):
         arrive(cot_pairs[s], ch.at[s, 0], ch.at[s, 1])
@@ -348,7 +358,7 @@
         return finished
 
     halves = [stage1(0), stage1(1)]
-    for c in (*halves[0][1], *cot_pairs[1], *halves[1][1]):
+    for c in (*halves[0][1], *halves[1][1]):
         c.start()
     second_own(0, halves[0][0])
     acc2[:, 0:192] = second_grad(0)
@@ -376,6 +386,8 @@
     scattered = exchange(0, slab_group, lambda slab, c: pack2.at[pl.ds(slab * tp, tp)], r1.at[i1])
 
     acc1[...] = jnp.zeros_like(acc1)
+    for s in range(2):
+        after_own(s)
     for s in range(2):
         second_beside(s, halves[s][1])
         stage3(s)
@@ -421,6 +433,7 @@
     over()
     out_s1[...] = jnp.sum(q1[...], axis=0)
     gathered()
+    sent_off(*(h[0] for h in halves), *(h[1] for h in halves), *cot_pairs)
     out_s2[...] = res[...].reshape(128, 128)
 
 
@@ -487,7 +500,7 @@
                 pltpu.VMEM((2, 2, 32, 8, 128), BF16),
                 pltpu.VMEM((2, 2, 32, 8, 128), BF16),
                 pltpu.VMEM((4, 256, 128), F32),
-                pltpu.VMEM((512, 128), F32),
+                pltpu.VMEM((2, 512, 128), F32),
                 pltpu.VMEM((2, 10, 64, 128), BF16),
                 pltpu.VMEM((2, 18, 64, 256), BF16),
                 pltpu.VMEM((2, 3072, 128), BF16),

time: 47.2 us -> 45.6 us (0.966)
  Pallas kernels: 46.5 us -> 44.9 us
    pallas_call x1, Pallas kernels: 45.6 us -> 44 us  [body(): pl.pallas_call(functools.partial(kernel, sizes), out_shape=(pltpu.VMEM((2...]
where the time goes in v5:
time: 45.6 us; the launch traced here: 45.5 us
  Pallas kernels  44.9 us (98%)
  between operations  0.64 us (1%)
    pallas_call x1, Pallas kernels, body(): pl.pallas_call(functools.partial(kernel, sizes), out_shape=(pltpu.VMEM((2...  44 us

profile of v5, /device:TPU:1, one launch (start us, length us, event | category | flops | bytes accessed | tf_op | source)
XLA Modules:
  0.0 45.5 jit_solution(11453938514700097142)
XLA Ops:
  0.6 44.0 %shard_map.75 = (bf16[2,32,2,8,128]{4,3,2,1,0:T(8,128)(2,1)S(1)}, bf16[2,16,2,8,128]{4,3,2,1,0:T(8,128)(2,1)S(1)}, f32[16,128]{1,0:T(8,128)S(1)}, f32[128,128]{1,0:T(8,128)S(1)}) custom-call(bf16[2,4,4,16,256]{4,3,2,1,0:T(8,128)(2,1)} %vol.1, bf16[3,3,3,4,16]{4,3,2,1,0:T(4,128)(2,1)} %bitcast.5, bf16[3,3,3,16,32]{4,3,2,1,0:T(8,128)(2,1)} %bitcast.4, ...), custom_call_target="tpu_custom_call" | custom-call | tf_op jit(solution)/shard_map/pallas_call | solution.py:482
  44.7 0.9 %shard_map.76 = (bf16[2,32,2,8,128]{4,3,2,1,0:T(8,128)(2,1)}, bf16[2,16,2,8,128]{4,3,2,1,0:T(8,128)(2,1)}, f32[3,3,3,4,16]{4,3,2,1,0:T(4,128)}, f32[3,3,3,16,32]{4,3,2,1,0:T(8,128)}) custom-call(bf16[2,32,2,8,128]{4,3,2,1,0:T(8,128)(2,1)S(1)} %get-tuple-element.12.act, bf16[2,16,2,8,128]{4,3,2,1,0:T(8,128)(2,1)S(1)} %get-tuple-element.13.pg, ...), custom_call_target="tpu_custom_call" | custom-call | tf_op jit(solution)/shard_map/pallas_call | solution.py:535

commit v6 on v5

--- a/solution.py
+++ b/solution.py
@@ -209,7 +209,7 @@
         arrive(halos[s], vbuf.at[s, 0], vbuf.at[s, 5])
         planes = vbuf[s].reshape(384, 256).astype(F32)
         for half in range(2):
-            vf[half] = planes[:, 128 * half : 128 * half + 128]
+            vf[half, 0:384] = planes[:, 128 * half : 128 * half + 128]
         for y in range(16):
             v = jnp.concatenate([vf[half, pl.ds(y, 24, stride=16), :] for half in range(2)], axis=1)
             before, after = shifts(v)
@@ -276,7 +276,7 @@
 
     def second_own(s, near):
         for x in range(2):
-            cotf[x + 1] = cotb[s, x].reshape(256, 128).astype(F32)
+            cotf[x + 1, 0:256] = cotb[s, x].reshape(256, 128).astype(F32)
         arrive(near, ph.at[s, 0, 1], ph.at[s, 1, 0])
         fill(s, ((0, 1, 1), (1, 0, 4)))
         for j, pre in enumerate(convolved(s, a2[...], 48, 64)):
@@ -287,14 +287,14 @@
             db[s, j + 1] = (jnp.concatenate(got, axis=0) * sl).astype(BF16)
 
     def after_own(s):
-        out_act[s] = actf[s].reshape(32, 2, 8, 128).astype(BF16)
+        out_act[s] = actf[s, 0:512].reshape(32, 2, 8, 128).astype(BF16)
         for j in range(8):
             spread_delta(s, j, db[s, j + 1], ((0, 64, 32),))
 
     def second_beside(s, far):
         arrive(cot_pairs[s], ch.at[s, 0], ch.at[s, 1])
         for side in range(2):
-            cotf[3 * side] = ch[s, side].reshape(256, 128).astype(F32)
+            cotf[3 * side, 0:256] = ch[s, side].reshape(256, 128).astype(F32)
         arrive(far, ph.at[s, 0, 0], ph.at[s, 1, 1])
         fill(s, ((0, 0, 0), (1, 1, 5)))
         low = convolved(s, a2h[0], 0, 32)
@@ -328,7 +328,7 @@
             up = jnp.concatenate([up[0:16], up[0:16], up[16:32], up[16:32]], axis=0)
             for y in (2 * j, 2 * j + 1):
                 fd[s, y + 1] = (up * slope[s, y * 64 : y * 64 + 64, :]).astype(BF16)
-        out_pg[s] = bkf[...].reshape(16, 2, 8, 128).astype(BF16)
+        out_pg[s] = bkf[0:256].reshape(16, 2, 8, 128).astype(BF16)
 
     def first_grad(s):
         total = None
@@ -362,6 +362,7 @@
         c.start()
     second_own(0, halves[0][0])
     acc2[:, 0:192] = second_grad(0)
+    after_own(0)
     second_own(1, halves[1][0])
     acc2[:, 0:192] += second_grad(1)
 
@@ -386,8 +387,7 @@
     scattered = exchange(0, slab_group, lambda slab, c: pack2.at[pl.ds(slab * tp, tp)], r1.at[i1])
 
     acc1[...] = jnp.zeros_like(acc1)
-    for s in range(2):
-        after_own(s)
+    after_own(1)
     for s in range(2):
         second_beside(s, halves[s][1])
         stage3(s)
@@ -491,7 +491,7 @@
             out_specs=(vmem,) * 4,
             scratch_shapes=[
                 pltpu.VMEM((2, 6, 4, 16, 256), BF16),
-                pltpu.VMEM((2, 384, 128), F32),
+                pltpu.VMEM((2, 400, 128), F32),
                 pltpu.VMEM((2, 1456, 256), BF16),
                 pltpu.VMEM((2, 1024, 256), F32),
                 pltpu.VMEM((2, 2, 8, 16, 128), BF16),
@@ -499,12 +499,12 @@
                 pltpu.VMEM((2, 2304, 128), BF16),
                 pltpu.VMEM((2, 2, 32, 8, 128), BF16),
                 pltpu.VMEM((2, 2, 32, 8, 128), BF16),
-                pltpu.VMEM((4, 256, 128), F32),
-                pltpu.VMEM((2, 512, 128), F32),
+                pltpu.VMEM((4, 264, 128), F32),
+                pltpu.VMEM((2, 528, 128), F32),
                 pltpu.VMEM((2, 10, 64, 128), BF16),
                 pltpu.VMEM((2, 18, 64, 256), BF16),
                 pltpu.VMEM((2, 3072, 128), BF16),
-                pltpu.VMEM((256, 128), F32),
+                pltpu.VMEM((272, 128), F32),
                 pltpu.VMEM((3, 3, 3, 4, 16), BF16),
                 pltpu.VMEM((3, 3, 3, 16, 32), BF16),
                 pltpu.VMEM((256, 128), F32),

time: 45.6 us -> 45.6 us (level)
  no operation moved by 1% of the time
where the time goes in v6:
time: 45.6 us; the launch traced here: 45.5 us
  Pallas kernels  44.9 us (98%)
  between operations  0.64 us (1%)
    pallas_call x1, Pallas kernels, body(): pl.pallas_call(functools.partial(kernel, sizes), out_shape=(pltpu.VMEM((2...  44 us

profile of v6, /device:TPU:1, one launch (start us, length us, event | category | flops | bytes accessed | tf_op | source)
XLA Modules:
  0.0 45.5 jit_solution(9854007892243709906)
XLA Ops:
  0.6 44.0 %shard_map.75 = (bf16[2,32,2,8,128]{4,3,2,1,0:T(8,128)(2,1)S(1)}, bf16[2,16,2,8,128]{4,3,2,1,0:T(8,128)(2,1)S(1)}, f32[16,128]{1,0:T(8,128)S(1)}, f32[128,128]{1,0:T(8,128)S(1)}) custom-call(bf16[2,4,4,16,256]{4,3,2,1,0:T(8,128)(2,1)} %vol.1, bf16[3,3,3,4,16]{4,3,2,1,0:T(4,128)(2,1)} %bitcast.5, bf16[3,3,3,16,32]{4,3,2,1,0:T(8,128)(2,1)} %bitcast.4, ...), custom_call_target="tpu_custom_call" | custom-call | tf_op jit(solution)/shard_map/pallas_call | solution.py:482
  44.6 0.9 %shard_map.76 = (bf16[2,32,2,8,128]{4,3,2,1,0:T(8,128)(2,1)}, bf16[2,16,2,8,128]{4,3,2,1,0:T(8,128)(2,1)}, f32[3,3,3,4,16]{4,3,2,1,0:T(4,128)}, f32[3,3,3,16,32]{4,3,2,1,0:T(8,128)}) custom-call(bf16[2,32,2,8,128]{4,3,2,1,0:T(8,128)(2,1)S(1)} %get-tuple-element.12.act, bf16[2,16,2,8,128]{4,3,2,1,0:T(8,128)(2,1)S(1)} %get-tuple-element.13.pg, ...), custom_call_target="tpu_custom_call" | custom-call | tf_op jit(solution)/shard_map/pallas_call | solution.py:535
